TPU v7x, 256 devices: a whole 4x4x8 slice. The times are simulated.
256 devices in a mesh: rows: 256 (over x, y, z, core).
Axes of the slice: x: 4, y: 4, z: 8, core: 2. Of those that a mesh axis runs over, the one named last changes fastest.
Arguments:
- features: float32 [1048576, 64], P('rows'), may hold values from -6 to 6
- prev_factors: float32 [1048576, 384], P('rows'), may hold values from -0.15 to 0.15
- inv_scales: float32 [64], replicated, may hold values from 0.005 to 0.03
- noise: float32 [1], replicated, may hold values from 1 to 2
- pivot_owner: int32 [2, 64], replicated, may hold values from 0 to 255, as said below
- pivot_local: int32 [2, 64], replicated, may hold values from 0 to 4095, as said below
Outputs:
- new_factors: float32 [1048576, 128], P('rows')
- residual_diag: float32 [1048576], P('rows')
- trace: float32 [1], replicated
Inputs may be any that keep to these rules, and one draw needn't show every extreme that they name: `pivot_owner`: device indices; low indices hold more pivots. `pivot_local`: all 128 pivot rows are distinct within their devices' rows, so all pivots are distinct.
All inputs are finite; a program needn't handle non-finite values.
Results may differ from a plain program's by a relative error of at most 0.00017.
Values sent between devices are 32-bit elements; how exact they have to be, the bound alone decides.
No kernel may reach another device: no remote copies, remote signals or barrier semaphores. Data moves between devices by JAX's collectives and lax.ppermute only.
A program may use at most 64 MiB of HBM per device.

v0:
```python
import jax
import jax.numpy as jnp
from jax import lax
from jax.sharding import PartitionSpec as P

HIGH = lax.Precision.HIGHEST


def kernel_block(left, right, weights):
    scaled = left * weights
    cross = jnp.dot(scaled, right.T, precision=HIGH, preferred_element_type=jnp.float32)
    left_sq = jnp.sum(scaled * left, axis=1)
    right_sq = jnp.sum(right * right * weights, axis=1)
    return jnp.exp(-0.5 * (left_sq[:, None] + right_sq[None, :] - 2.0 * cross))


def hit_table(owners, places, local_rows, myself):
    row_ids = jnp.arange(local_rows, dtype=jnp.int32)
    return ((row_ids[:, None] == places[None, :]) & (owners[None, :] == myself)).astype(jnp.float32)


def select_rows(table, parts):
    pieces = [
        jnp.dot(table.T, part_now, precision=HIGH, preferred_element_type=jnp.float32)
        for part_now in parts
    ]
    return jnp.concatenate(pieces, axis=1)


def local(features, prev_factors, inv_scales, noise, pivot_owner, pivot_local):
    local_rows = features.shape[0]
    feat = features.shape[1]
    prev_width = prev_factors.shape[1]
    panel_size = pivot_owner.shape[1]
    panel_count = pivot_owner.shape[0]
    myself = lax.axis_index("rows")
    blocks = []
    for panel in range(panel_count):
        owners = pivot_owner[panel]
        places = pivot_local[panel]
        table = hit_table(owners, places, local_rows, myself)
        fetched = lax.psum(select_rows(table, [features, prev_factors] + blocks), "rows")
        piv_x = fetched[:, :feat]
        piv_fac = fetched[:, feat:]
        cols = kernel_block(features, piv_x, inv_scales) + noise[0] * table
        cols = cols - jnp.dot(
            prev_factors,
            piv_fac[:, :prev_width].T,
            precision=HIGH,
            preferred_element_type=jnp.float32,
        )
        pivot_block = kernel_block(piv_x, piv_x, inv_scales) + noise[0] * jnp.eye(
            panel_size, dtype=jnp.float32
        )
        piv_prev = piv_fac[:, :prev_width]
        pivot_block = pivot_block - jnp.dot(
            piv_prev, piv_prev.T, precision=HIGH, preferred_element_type=jnp.float32
        )
        for order, earlier in enumerate(blocks):
            offset = prev_width + order * panel_size
            piv_e = piv_fac[:, offset : offset + panel_size]
            cols = cols - jnp.dot(
                earlier, piv_e.T, precision=HIGH, preferred_element_type=jnp.float32
            )
            pivot_block = pivot_block - jnp.dot(
                piv_e, piv_e.T, precision=HIGH, preferred_element_type=jnp.float32
            )
        lower = jnp.linalg.cholesky(pivot_block)
        fresh = lax.linalg.triangular_solve(
            lower, cols, left_side=False, lower=True, transpose_a=True
        )
        blocks.append(fresh)
    new_factors = jnp.concatenate(blocks, axis=1)
    residual_diag = (
        1.0
        + noise[0]
        - jnp.sum(prev_factors * prev_factors, axis=1)
        - jnp.sum(new_factors * new_factors, axis=1)
    )
    trace = lax.psum(jnp.sum(residual_diag), "rows").reshape(1)
    return (new_factors, residual_diag, trace)


def solution(mesh):
    placed = (P("rows", None), P("rows", None), P(), P(), P(), P())
    return jax.shard_map(
        local,
        mesh=mesh,
        in_specs=placed,
        out_specs=(P("rows", None), P("rows"), P()),
        check_vma=False,
    )
```

profile of v0, /device:TPU:1, one launch (start us, length us, event | category | flops | bytes accessed | tf_op | source)
XLA Modules:
  0.0 655.7 jit_solution(11122831684328428246)
XLA Ops:
  7.2 0.0 all-reduce.3.cloned.1.call-start
  7.2 0.8 slice_bitcast_fusion
  8.0 0.8 compare_bitcast_fusion
  8.7 0.0 copy-start
  8.7 6.0 fusion.11
  14.8 0.0 copy-done
  14.8 1.3 fusion.33
  16.1 0.8 pad_maximum_fusion.1
  16.8 0.0 all-reduce.3.cloned.1.call-update
  16.9 0.5 all-reduce.5.cloned.1.call-start
  17.4 0.0 copy-start.3
  17.4 5.9 fusion.15
  23.3 1.3 fusion.22
  24.6 0.0 copy-done.3
  24.6 0.2 fusion.32
  25.5 236.1 %all-reduce.3.cloned.1.call-done = f32[64,448]{1,0:T(8,128)} async-done(((f32[64,448]{1,0:T(8,128)}), f32[64,448]{1,0:T(8,128)}) %all-reduce.3.cloned.1.call-update) | async-done | bytes 114704 | tf_op jit(solution)/shard_map/psum | solution.py:42
  261.6 0.9 fusion.55
  262.5 1.0 fusion.31
  263.5 1.3 convolution_subtract_fusion.3
  264.8 0.1 copy.11
  264.9 5.8 cholesky.44
  270.8 0.6 compare_reduce_fusion.1
  271.5 0.7 fusion.53
  272.1 4.9 custom-call.6
  277.0 0.0 copy-start.2
  277.0 5.2 fusion.9
  282.2 0.0 copy-done.2
  282.2 8.3 %fusion.5 = f32[4096,64]{1,0:T(8,128)S(1)} fusion(f32[4096,64]{1,0:T(8,128)S(1)} %fusion.9, f32[4096,384]{1,0:T(8,128)} %param.10, f32[64,448]{1,0:T(8,128)S(1)} %copy-done.2), kind=kOutput, calls=%fused_computation.10 | convolution fusion | flops 1208221696 | bytes 9535488 | tf_op jit(solution)/shard_map/dot_general | solution.py:46
  290.5 2.3 convolution_bitcast_fusion.3
  292.8 1.3 fusion.20
  294.1 0.8 pad_maximum_fusion.2
  294.9 0.0 all-reduce.5.cloned.1.call-update
  294.9 3.4 multiply_reduce_fusion
  298.3 235.2 %all-reduce.5.cloned.1.call-done = f32[64,512]{1,0:T(8,128)} async-done(((f32[64,512]{1,0:T(8,128)}), f32[64,512]{1,0:T(8,128)}) %all-reduce.5.cloned.1.call-update) | async-done | bytes 131088 | tf_op jit(solution)/shard_map/psum | solution.py:42
  533.5 0.9 fusion.56
  534.4 1.0 fusion.27
  535.4 1.3 convolution_subtract_fusion.2
  536.7 1.1 convolution_subtract_fusion.1
  537.8 0.1 copy.15
  537.9 5.8 cholesky.55
  543.8 0.6 compare_reduce_fusion
  544.4 0.7 fusion.54
  545.1 4.9 custom-call.7
  550.0 0.0 copy-start.1
  550.0 5.2 fusion.4
  555.2 0.0 copy-done.1
  555.2 8.3 %fusion = f32[4096,64]{1,0:T(8,128)S(1)} fusion(f32[4096,64]{1,0:T(8,128)S(1)} %fusion.4, f32[4096,384]{1,0:T(8,128)} %param.10, f32[64,512]{1,0:T(8,128)S(1)} %copy-done.1), kind=kOutput, calls=%fused_computation.3 | convolution fusion | flops 1208221696 | bytes 9535488 | tf_op jit(solution)/shard_map/dot_general | solution.py:46
  563.6 3.5 convolution_subtract_fusion
  567.1 2.3 convolution_bitcast_fusion.2
  569.4 0.4 multiply_reduce_fusion.1
  569.8 1.8 copy.16
  571.6 1.2 fusion.69
  572.8 75.9 %psum.23 = f32[1]{0:T(128)} all-reduce(f32[1]{0:T(128)} %bitcast.15), channel_id=1, replica_groups=mesh['rows'=256] {'rows'}, use_global_device_ids=true, to_apply=%region_12.15 | all-reduce | flops 1 | bytes 8 | tf_op jit(solution)/shard_map/psum | solution.py:80
  (4 shorter events, 0.1 us)
Async XLA Ops:
  7.2 254.5 %all-reduce.3.cloned.1.call-start = ((), (), s32[]{:S(2)}) async-start(), calls=%async_computation | async-start | bytes 262144 | tf_op jit(solution)/shard_map/psum | solution.py:42
  8.7 6.0 copy-start
  16.9 516.6 %all-reduce.5.cloned.1.call-start = ((), (), s32[]{:S(2)}) async-start(), calls=%async_computation.1 | async-start | bytes 262144 | tf_op jit(solution)/shard_map/psum | solution.py:42
  17.4 7.3 %copy-start.3 = (f32[64]{0:T(128)S(1)}, f32[64]{0:T(128)}, u32[]{:S(2)}) copy-start(f32[64]{0:T(128)} %param.11) | copy-start | bytes 772
  277.0 5.2 copy-start.2
  550.0 5.2 copy-start.1
Sparse Core Ops, SparseCore 0:
  17.0 244.6 all-reduce.2
  295.0 238.4 all-reduce.4
where the time goes:
time: 660 us; the launch traced here: 656 us
  waiting for transfers between devices  471 us (71%)
  blocking collectives  75.9 us (12%)
  matrix products  56.7 us (9%)
  other arithmetic  33.3 us (5%)
  between operations  15.2 us (2%)
    psum x2, waiting for transfers between devices, local(): lax.psum(select_rows(table, [features, prev_factors] + blocks), 'rows')  471 us
    psum x1, blocking collectives, local(): trace = lax.psum(jnp.sum(residual_diag), 'rows').reshape(1)  75.9 us
    dot_general x2, matrix products, local(): jnp.dot(prev_factors, piv_fac[:, :prev_width].T, precision=HIGH, preferre...  16.6 us
    dot_general x5, matrix products, select_rows(): jnp.dot(table.T, part_now, precision=HIGH, preferred_element_type=jnp.flo...  15.8 us
  transfers between devices with their start and end apart: 2, of which 2 were waited for; matrix products, arithmetic and copies ran while one was open for 2% of the time, Pallas kernels for 0%

commit v1 on v0

v1 whole, which is shorter than its diff:
```python
import functools

import jax
import jax.numpy as jnp
from jax import lax
from jax.experimental import pallas as pl
from jax.experimental.pallas import tpu as pltpu
from jax.sharding import PartitionSpec as P

F32 = jnp.float32
BF16 = jnp.bfloat16
HIGH = lax.Precision.HIGHEST
VMEM = pl.BlockSpec(memory_space=pltpu.VMEM)
SMEM = pl.BlockSpec(memory_space=pltpu.SMEM)
ANY = pl.BlockSpec(memory_space=pl.ANY)
NT = (((1,), (1,)), ((), ()))


def groups_of(total, fields):
    found = {}
    for index in range(total):
        key = index
        for stride, size in fields:
            key -= ((index // stride) % size) * stride
        found.setdefault(key, []).append(index)
    return list(found.values())


def exchange(blocks, groups):
    return lax.all_to_all(blocks, "rows", 0, 0, axis_index_groups=groups, tiled=True)


def pick_kernel(me_ref, owner_ref, place_ref, feat_ref, prev_ref, out_ref, feat_rows, prev_rows, sems):
    out_ref[...] = jnp.zeros_like(out_ref)
    pivots = owner_ref.shape[0]
    feat = feat_ref.shape[1]
    me = me_ref[0]

    def copies(pivot):
        base = pl.multiple_of((place_ref[pivot] // 8) * 8, 8)
        return (
            pltpu.make_async_copy(feat_ref.at[pl.ds(base, 8)], feat_rows.at[pivot], sems.at[0, pivot]),
            pltpu.make_async_copy(prev_ref.at[pl.ds(base, 8)], prev_rows.at[pivot], sems.at[1, pivot]),
        )

    def start(pivot, carry):
        @pl.when(owner_ref[pivot] == me)
        def _():
            for copy in copies(pivot):
                copy.start()

        return carry

    def finish(pivot, carry):
        @pl.when(owner_ref[pivot] == me)
        def _():
            for copy in copies(pivot):
                copy.wait()
            row = lax.rem(place_ref[pivot], 8)
            slot = pivot // 8
            inner = lax.rem(pivot, 8)
            x = feat_rows[pivot]
            fac = prev_rows[pivot]
            x = jnp.concatenate([x, jnp.zeros((8, 128 - feat), F32)], axis=1)
            for half, rows in ((0, jnp.concatenate([x, fac[:, :128]], axis=1)), (1, fac[:, 128:])):
                sub = lax.broadcasted_iota(jnp.int32, rows.shape, 0)
                only = jnp.sum(jnp.where(sub == row, rows, 0.0), axis=0, keepdims=True)
                out_ref[slot, half] = jnp.where(sub == inner, only, out_ref[slot, half])

        return carry

    lax.fori_loop(0, pivots, start, 0)
    lax.fori_loop(0, pivots, finish, 0)


def split2(value):
    high = value.astype(BF16)
    return high, (value - high.astype(F32)).astype(BF16)


def split3(value):
    high = value.astype(BF16)
    rest = value - high.astype(F32)
    mid = rest.astype(BF16)
    return high, mid, (rest - mid.astype(F32)).astype(BF16)


def invert_factor(block):
    size = block.shape[0]
    rows = [block[8 * at : 8 * at + 8] for at in range(size // 8)]
    lane = lax.broadcasted_iota(jnp.int32, (8, size), 1)
    sub = lax.broadcasted_iota(jnp.int32, (8, size), 0)
    for step in range(size - 1):
        home, inner = divmod(step, 8)
        here = lane == step
        pivot_row = rows[home][inner : inner + 1, :]
        inverse = 1.0 / pivot_row[:, step : step + 1]
        scaled = jnp.where(here[:1], 1.0, pivot_row) * inverse
        for at in range(home, size // 8):
            if at == home and inner == 7:
                continue
            now = rows[at]
            column = now[:, step : step + 1]
            if at == home:
                column = jnp.where(sub[:, :1] > inner, column, 0.0)
                kept = jnp.where(here & (sub > inner), 0.0, now)
            else:
                kept = jnp.where(here, 0.0, now)
            rows[at] = kept - column * scaled
    done = jnp.concatenate(rows, axis=0)
    row_id = lax.broadcasted_iota(jnp.int32, (size, size), 0)
    col_id = lax.broadcasted_iota(jnp.int32, (size, size), 1)
    diag = jnp.sum(jnp.where(row_id == col_id, done, 0.0), axis=1, keepdims=True)
    unit = jnp.where(row_id == col_id, 1.0, jnp.where(col_id < row_id, done, 0.0))
    return unit * lax.rsqrt(diag)


def panel_kernel(
    me_ref, noise_ref, owner_ref, place_ref, scales_ref, pivots_ref, feat_ref, prev_ref,
    new_ref, resid_ref, part_ref, cols_ref, squares_ref, *, tile,
):
    points, feat = feat_ref.shape
    width = prev_ref.shape[1]
    size = owner_ref.shape[1]
    noise = noise_ref[0]
    scales = scales_ref[...]
    low = pivots_ref[:, 0].reshape(size, 256)
    piv_x = low[:, :feat]
    piv_f = jnp.concatenate([low[:, 128:], pivots_ref[:, 1].reshape(size, 256)], axis=1)

    piv_s = piv_x * scales
    cross = lax.dot_general(piv_s, piv_x, NT, precision=HIGH, preferred_element_type=F32)
    squared = piv_s * piv_x
    left_sq = jnp.sum(squared, axis=1, keepdims=True)
    right_sq = lax.dot_general(
        jnp.ones((8, feat), F32), squared, NT, precision=HIGH, preferred_element_type=F32
    )[:1]
    row_id = lax.broadcasted_iota(jnp.int32, (size, size), 0)
    col_id = lax.broadcasted_iota(jnp.int32, (size, size), 1)
    block = jnp.exp(-0.5 * (left_sq + right_sq - 2.0 * cross))
    block = block + jnp.where(row_id == col_id, noise, 0.0)
    block = block - lax.dot_general(piv_f, piv_f, NT, precision=HIGH, preferred_element_type=F32)
    inverse = invert_factor(block)

    mine = jnp.where(owner_ref[...] == me_ref[0], place_ref[...], -1)
    fac_high, fac_low = split2(piv_f)
    fac_rhs = jnp.concatenate(
        [jnp.concatenate([fac_high, fac_high], axis=1), jnp.concatenate([fac_low, fac_low], axis=1)],
        axis=0,
    )
    x_high, x_mid, x_low = split3(piv_x)
    x_rhs = jnp.concatenate([x_high, x_mid], axis=0)

    def columns(at, carry):
        base = pl.multiple_of(at * tile, tile)
        here = pl.ds(base, tile)
        x = feat_ref[here, :]
        s = x * scales
        left = jnp.sum(s * x, axis=1, keepdims=True)
        s_high, s_mid, s_low = split3(s)
        two = lax.dot_general(s_high, x_rhs, NT, preferred_element_type=F32)
        two = two + lax.dot_general(s_mid, x_rhs, NT, preferred_element_type=F32)
        cross = two[:, :size] + two[:, size:]
        cross = cross + lax.dot_general(s_high, x_low, NT, preferred_element_type=F32)
        cross = cross + lax.dot_general(s_low, x_high, NT, preferred_element_type=F32)
        kern = jnp.exp(-0.5 * (left + right_sq - 2.0 * cross))
        ids = lax.broadcasted_iota(jnp.int32, (tile, size), 0) + base
        kern = kern + jnp.where(ids == mine, noise, 0.0)
        fac = prev_ref[here, :]
        high, low_part = split2(fac)
        both = lax.dot_general(
            jnp.concatenate([high, low_part], axis=1), fac_rhs, NT, preferred_element_type=F32
        )
        cols_ref[here, :] = kern - (both[:, :size] + both[:, size:])
        total = fac[:, :128] * fac[:, :128]
        for start in range(128, width, 128):
            total = total + fac[:, start : start + 128] * fac[:, start : start + 128]
        squares_ref[here, :] = total
        return carry

    lax.fori_loop(0, points // tile, columns, 0)

    inv_high, inv_low = split2(inverse)
    inv_rhs = jnp.concatenate(
        [jnp.concatenate([inv_high, inv_high], axis=1), jnp.concatenate([inv_low, inv_low], axis=1)],
        axis=0,
    )

    def finish(at, total):
        here = pl.ds(pl.multiple_of(at * tile, tile), tile)
        high, low_part = split2(cols_ref[here, :])
        both = lax.dot_general(
            jnp.concatenate([high, low_part], axis=1), inv_rhs, NT, preferred_element_type=F32
        )
        new = both[:, :size] + both[:, size:]
        new_ref[here, :] = new
        gone = squares_ref[here, :] + new * new
        for sub_at in range(tile // 128):
            flipped = gone[sub_at * 128 : (sub_at + 1) * 128, :].T
            row = 1.0 + noise - jnp.sum(flipped, axis=0, keepdims=True)
            resid_ref[pl.ds(at * (tile // 128) + sub_at, 1), :] = row
            total = total + row
        return total

    total = lax.fori_loop(0, points // tile, finish, jnp.zeros((1, 128), F32))
    part_ref[...] = jnp.broadcast_to(jnp.sum(total, axis=1, keepdims=True), part_ref.shape)


def local(devices, features, prev_factors, inv_scales, noise, pivot_owner, pivot_local):
    points, feat = features.shape
    width = prev_factors.shape[1]
    pivots = pivot_owner.size
    me = lax.axis_index("rows").astype(jnp.int32).reshape(1)
    owner = pivot_owner.reshape(pivots)
    place = pivot_local.reshape(pivots)
    layer = groups_of(devices, ((1, 2), (16, 16)))
    column = groups_of(devices, ((2, 8),))

    picked = pl.pallas_call(
        pick_kernel,
        out_shape=jax.ShapeDtypeStruct((16, 2, 8, 256), F32),
        in_specs=[SMEM, SMEM, SMEM, ANY, ANY],
        out_specs=VMEM,
        scratch_shapes=[
            pltpu.VMEM((pivots, 8, feat), F32),
            pltpu.VMEM((pivots, 8, width), F32),
            pltpu.SemaphoreType.DMA((2, pivots)),
        ],
        name="pick",
    )(me, owner, place, features, prev_factors)

    part = exchange(picked.reshape(32, 8, 256), layer).sum(0)
    part = exchange(jnp.broadcast_to(part[None], (8, 8, 256)), column).sum(0)
    rows = exchange(jnp.broadcast_to(part[None], (32, 8, 256)), layer)

    new_factors, resid, part = pl.pallas_call(
        functools.partial(panel_kernel, tile=256),
        out_shape=(
            jax.ShapeDtypeStruct((points, pivots), F32),
            jax.ShapeDtypeStruct((points // 128, 128), F32),
            jax.ShapeDtypeStruct((devices, 128), F32),
        ),
        in_specs=[SMEM, SMEM, VMEM, VMEM, VMEM, VMEM, VMEM, VMEM],
        out_specs=(VMEM, VMEM, VMEM),
        scratch_shapes=[pltpu.VMEM((points, pivots), F32), pltpu.VMEM((points, 128), F32)],
        compiler_params=pltpu.CompilerParams(vmem_limit_bytes=32 * 1024 * 1024),
        name="panel",
    )(
        me, noise, owner.reshape(1, pivots), place.reshape(1, pivots), inv_scales.reshape(1, feat),
        rows.reshape(16, 2, 8, 256), features, prev_factors,
    )
    sums = exchange(part.reshape(devices, 1, 128), None)
    trace = jnp.sum(sums[:, 0, 0]).reshape(1)
    return new_factors, resid.reshape(points), trace


def solution(mesh):
    placed = (P("rows", None), P("rows", None), P(), P(), P(), P())
    return jax.shard_map(
        functools.partial(local, mesh.shape["rows"]),
        mesh=mesh,
        in_specs=placed,
        out_specs=(P("rows", None), P("rows"), P()),
        check_vma=False,
    )
```

time: 660 us -> 109 us (0.17)
  waiting for transfers between devices: 471 us -> 8.27 us
  matrix products: 56.7 us -> 0 us
  Pallas kernels: 0 us -> 32.4 us
  other arithmetic: 33.3 us -> 0.91 us
  blocking collectives: 75.9 us -> 50.7 us
  between operations: 15.2 us -> 1.34 us
  local copies, waits for them, and re-layouts: 2.76 us -> 9.43 us
    psum x2 -> x0, waiting for transfers between devices: 471 us -> none  [local(): lax.psum(select_rows(table, [features, prev_factors] + blocks), 'rows')]
    psum x1 -> x0, blocking collectives: 75.9 us -> none  [local(): trace = lax.psum(jnp.sum(residual_diag), 'rows').reshape(1)]
    dot_general x15 -> x0, matrix products: 52.1 us -> none  [the longest x2 16.6 us: local(): jnp.dot(prev_factors, piv_fac[:, :prev_width].T, precision=HIGH, preferre...]
    all_to_all x0 -> x3, blocking collectives: none -> 50.7 us  [exchange(): lax.all_to_all(blocks, 'rows', 0, 0, axis_index_groups=groups, tiled=True)]
    pallas_call x0 -> x2, Pallas kernels: none -> 32.4 us  [the longest x1 24.1 us: local(): pl.pallas_call(functools.partial(panel_kernel, tile=256), out_shape=(jax....]
    another operation x10 -> x0, other arithmetic: 24.1 us -> none  [the longest x6 13 us: local(): lower = jnp.linalg.cholesky(pivot_block)]
    all_to_all x0 -> x1, waiting for transfers between devices: none -> 8.27 us  [exchange(): lax.all_to_all(blocks, 'rows', 0, 0, axis_index_groups=groups, tiled=True)]
  transfers between devices with their start and end apart: 2 -> 1, of which waited for: 2 -> 1; matrix products, arithmetic and copies ran while one was open for 2% -> 0% of each run, Pallas kernels for 0% -> 0%
where the time goes in v1:
time: 109 us; the launch traced here: 108 us
  blocking collectives  50.7 us (47%)
  Pallas kernels  32.4 us (30%)
  local copies, waits for them, and re-layouts  9.43 us (9%)
  waiting for transfers between devices  8.27 us (8%)
  starting transfers between devices  5.19 us (5%)
  between operations  1.34 us (1%)
    all_to_all x3, blocking collectives, exchange(): lax.all_to_all(blocks, 'rows', 0, 0, axis_index_groups=groups, tiled=True)  50.7 us
    pallas_call x1, Pallas kernels, local(): pl.pallas_call(functools.partial(panel_kernel, tile=256), out_shape=(jax....  24.1 us
    pallas_call x1, Pallas kernels, local(): pl.pallas_call(pick_kernel, out_shape=jax.ShapeDtypeStruct((16, 2, 8, 256...  8.29 us
    all_to_all x1, waiting for transfers between devices, exchange(): lax.all_to_all(blocks, 'rows', 0, 0, axis_index_groups=groups, tiled=True)  8.27 us
    unnamed x11, local copies, waits for them, and re-layouts  5.95 us
    all_to_all x1, starting transfers between devices, exchange(): lax.all_to_all(blocks, 'rows', 0, 0, axis_index_groups=groups, tiled=True)  5.19 us
  transfers between devices with their start and end apart: 1, of which 1 were waited for; matrix products, arithmetic and copies ran while one was open for 0% of the time, Pallas kernels for 0%

profile of v1, /device:TPU:1, one launch (start us, length us, event | category | flops | bytes accessed | tf_op | source)
XLA Modules:
  0.0 108.2 jit_solution(10176181873937638676)
XLA Ops:
  0.6 1.3 %reshape.37.owner_ref = s32[128]{0:T(128)} reshape(s32[2,64]{1,0:T(2,128)} %param.10) | data formatting | bytes 1024 | tf_op jit(solution)/shard_map/reshape | solution.py:214
  1.9 1.3 %reshape.38.place_ref = s32[128]{0:T(128)} reshape(s32[2,64]{1,0:T(2,128)} %param.11) | data formatting | bytes 1024 | tf_op jit(solution)/shard_map/reshape | solution.py:215
  3.2 3.2 %copy.14.feat_ref = f32[4096,64]{1,0:T(8,128)} copy(f32[4096,64]{0,1:T(8,128)} %param.6) | data formatting | bytes 2097152 | tf_op args[0]
  6.4 0.0 copy-start.3
  6.4 0.0 copy-start.4
  6.4 0.0 copy-start.1
  6.4 0.0 copy-start.2
  6.4 8.3 %pick.1 = f32[16,2,8,256]{3,2,1,0:T(8,128)} custom-call(s32[1]{0:T(128)} %bitcast.me_ref, s32[128]{0:T(128)} %reshape.37.owner_ref, s32[128]{0:T(128)} %reshape.38.place_ref, f32[4096,64]{1,0:T(8,128)} %copy.14.feat_ref, f32[4096,384]{1,0:T(8,128)} %prev_ref.3), custom_call_target="tpu_custom_call" | custom-call | tf_op jit(solution)/shard_map/pick/pallas_call | solution.py:219
  14.7 17.5 %all_to_all.20 = f32[32,8,256]{2,1,0:T(8,128)S(1)} all-to-all(f32[32,8,256]{2,1,0:T(8,128)} %bitcast.12), channel_id=1, replica_groups={{0,1,16,17,32,33,48,49,64,65,80,81,96,97,112,113,128,129,144,145,160,16..., dimensions={0} | all-to-all | bytes 524288 | tf_op jit(solution)/shard_map/all_to_all | solution.py:30
  32.3 15.2 %all_to_all.21 = f32[8,8,256]{2,1,0:T(8,128)S(1)} all-to-all(f32[8,8,256]{2,1,0:T(8,128)S(1)} %broadcast_in_dim.4), channel_id=1, replica_groups={{0,2,4,6,8,10,12,14},{1,3,5,7,9,11,13,15},{16,18,20,22,24,26,28,30},{17..., dimensions={0} | all-to-all | bytes 131072 | tf_op jit(solution)/shard_map/all_to_all | solution.py:30
  47.5 0.7 broadcast_in_dim.5
  48.2 5.2 %all-to-all-start.2 = ((f32[32,8,256]{2,1,0:T(8,128)}), f32[32,8,256]{2,1,0:T(8,128)S(1)}, u32[]{:S(2)}, u32[]{:S(2)}) async-start(f32[32,8,256]{2,1,0:T(8,128)} %broadcast_in_dim.5), calls=%async_computation.2 | async-start | bytes 524288 | tf_op jit(solution)/shard_map/all_to_all | solution.py:30
  53.4 0.0 copy-done.3
  53.4 0.1 reshape_reshape.6.owner_ref
  53.5 0.0 copy-done.4
  53.5 0.1 reshape_reshape.7.place_ref
  54.2 8.3 %all-to-all-done.2 = f32[32,8,256]{2,1,0:T(8,128)S(1)} async-done(((f32[32,8,256]{2,1,0:T(8,128)}), f32[32,8,256]{2,1,0:T(8,128)S(1)}, u32[]{:S(2)}, u32[]{:S(2)}) %all-to-all-start.2) | async-done | bytes 262176 | tf_op jit(solution)/shard_map/all_to_all | solution.py:30
  62.5 0.0 copy-done.1
  62.5 0.0 copy-done.2
  62.5 0.0 copy-start
  62.5 2.8 %copy-done = f32[4096,384]{1,0:T(8,128)S(1)} copy-done((f32[4096,384]{1,0:T(8,128)S(1)}, f32[4096,384]{1,0:T(8,128)}, u32[]{:S(2)}) %copy-start) | copy-done | bytes 6291480
  65.3 24.1 %panel.1 = (f32[4096,128]{1,0:T(8,128)}, f32[32,128]{1,0:T(8,128)}, f32[256,128]{1,0:T(8,128)S(1)}) custom-call(s32[1]{0:T(128)} %bitcast.me_ref, f32[1]{0:T(128)S(6)} %copy.17.noise_ref, s32[1,128]{1,0:T(1,128)S(1)} %reshape_reshape.6.owner_ref, s32[1,128]{1,0:T(1,128)S(1)} %reshape_reshape.7.place_ref, f32[1,64]{1,0:T(1,128)S(1)} %bitcast.11, ...), custom_call_target="tpu_custom_call" | custom-call | tf_op jit(solution)/shard_map/panel/pallas_call | solution.py:236
  89.4 18.0 %all_to_all.22 = f32[256,1,128]{2,1,0:T(1,128)S(1)} all-to-all(f32[256,1,128]{2,1,0:T(1,128)S(1)} %bitcast.10), channel_id=1, replica_groups=mesh['rows'=256] {'rows'}, dimensions={0} | all-to-all | bytes 262144 | tf_op jit(solution)/shard_map/all_to_all | solution.py:30
  107.3 0.9 slice_reduce_fusion
  (3 shorter events, 0.1 us)
Async XLA Ops:
  6.4 47.0 %copy-start.3 = (s32[2,64]{1,0:T(2,128)S(1)}, s32[2,64]{1,0:T(2,128)}, u32[]{:S(2)}) copy-start(s32[2,64]{1,0:T(2,128)} %param.10) | copy-start | bytes 1540
  6.4 47.1 %copy-start.4 = (s32[2,64]{1,0:T(2,128)S(1)}, s32[2,64]{1,0:T(2,128)}, u32[]{:S(2)}) copy-start(s32[2,64]{1,0:T(2,128)} %param.11) | copy-start | bytes 1540
  6.4 56.1 %copy-start.1 = (f32[4096,64]{1,0:T(8,128)S(1)}, f32[4096,64]{1,0:T(8,128)}, u32[]{:S(2)}) copy-start(f32[4096,64]{1,0:T(8,128)} %copy.14.feat_ref) | copy-start | bytes 3145732
  6.4 56.1 %copy-start.2 = (f32[64]{0:T(128)S(1)}, f32[64]{0:T(128)}, u32[]{:S(2)}) copy-start(f32[64]{0:T(128)} %param.8) | copy-start | bytes 772
  48.2 14.3 %all-to-all-start.2 = ((f32[32,8,256]{2,1,0:T(8,128)}), f32[32,8,256]{2,1,0:T(8,128)S(1)}, u32[]{:S(2)}, u32[]{:S(2)}) async-start(f32[32,8,256]{2,1,0:T(8,128)} %broadcast_in_dim.5), calls=%async_computation.2 | async-start | bytes 524288 | tf_op jit(solution)/shard_map/all_to_all | solution.py:30
  62.5 2.8 %copy-start = (f32[4096,384]{1,0:T(8,128)S(1)}, f32[4096,384]{1,0:T(8,128)}, u32[]{:S(2)}) copy-start(f32[4096,384]{1,0:T(8,128)} %prev_ref.3) | copy-start | bytes 18874372

commit v2 on v0

v2 whole, which is shorter than its diff:
```python
import functools

import jax
import jax.numpy as jnp
from jax import lax
from jax.experimental import pallas as pl
from jax.experimental.pallas import tpu as pltpu
from jax.sharding import PartitionSpec as P

F32 = jnp.float32
BF16 = jnp.bfloat16
HIGH = lax.Precision.HIGHEST
VMEM = pl.BlockSpec(memory_space=pltpu.VMEM)
SMEM = pl.BlockSpec(memory_space=pltpu.SMEM)
ANY = pl.BlockSpec(memory_space=pl.ANY)
HBM = pl.BlockSpec(memory_space=pltpu.HBM)
NT = (((1,), (1,)), ((), ()))


def groups_of(total, fields):
    found = {}
    for index in range(total):
        key = index
        for stride, size in fields:
            key -= ((index // stride) % size) * stride
        found.setdefault(key, []).append(index)
    return list(found.values())


def exchange(blocks, groups):
    return lax.all_to_all(blocks, "rows", 0, 0, axis_index_groups=groups, tiled=True)


def pick_kernel(
    owner_hbm, place_hbm, feat_hbm, prev_hbm, out_ref, owner_ref, place_ref, feat_part, prev_part, found,
    table_sems, sems,
):
    tables = (
        pltpu.make_async_copy(owner_hbm, owner_ref, table_sems.at[0]),
        pltpu.make_async_copy(place_hbm, place_ref, table_sems.at[1]),
    )
    for copy in tables:
        copy.start()
    out_ref[...] = jnp.zeros_like(out_ref)
    feat_part[...] = jnp.zeros_like(feat_part)
    panels, panel = owner_ref.shape
    feat = feat_hbm.shape[0]
    slots = feat_part.shape[0]
    me = lax.axis_index("rows")
    for copy in tables:
        copy.wait()
    count = jnp.int32(0)
    for pivot in range(panels * panel):
        found[count] = pivot
        count = count + (owner_ref[pivot // panel, pivot % panel] == me).astype(jnp.int32)

    def place_of(at):
        pivot = found[at]
        return pivot, place_ref[pivot // panel, lax.rem(pivot, panel)]

    def copies(at, place):
        wide = pl.ds(pl.multiple_of((place // 128) * 128, 128), 128)
        rows = pl.ds(pl.multiple_of((place // 8) * 8, 8), 8)
        slot = lax.rem(at, slots)
        return (
            pltpu.make_async_copy(feat_hbm.at[:, wide], feat_part.at[slot], sems.at[0, slot]),
            pltpu.make_async_copy(prev_hbm.at[rows, :], prev_part.at[slot], sems.at[1, slot]),
        )

    def start(at, carry):
        for copy in copies(at, place_of(at)[1]):
            copy.start()
        return carry

    def land(at, carry):
        for copy in copies(at, place_of(at)[1]):
            copy.wait()
        return carry

    sub = lax.broadcasted_iota(jnp.int32, (8, 128), 0)
    lane = lax.broadcasted_iota(jnp.int32, (8, 128), 1)
    wide_sub = lax.broadcasted_iota(jnp.int32, (8, 256), 0)
    fac_sub = lax.broadcasted_iota(jnp.int32, prev_part.shape[1:], 0)

    def batch(at, carry):
        first = at * slots
        last = jnp.minimum(first + slots, count)
        lax.fori_loop(first, last, start, 0)
        lax.fori_loop(first, last, land, 0)
        homes, xs, facs = [], 0.0, []
        for slot in range(slots):
            used = first + slot < last
            pivot, place = place_of(jnp.where(used, first + slot, first))
            homes.append((pivot // 8, jnp.where(used, lax.rem(pivot, 8), -1)))
            only = jnp.where((sub == slot) & (lane == lax.rem(place, 128)), 1.0, 0.0)
            xs = xs + lax.dot_general(only, feat_part[slot], NT, precision=HIGH, preferred_element_type=F32)
            fac = jnp.where(fac_sub == lax.rem(place, 8), prev_part[slot], 0.0)
            facs.append(jnp.sum(fac, axis=0, keepdims=True))
        xs = jnp.concatenate([xs, jnp.zeros((slots, 128 - feat), F32)], axis=1)
        for slot, (home, inner) in enumerate(homes):
            here = wide_sub == inner
            left = jnp.concatenate([xs[slot : slot + 1], facs[slot][:, :128]], axis=1)
            out_ref[home, 0] = jnp.where(here, left, out_ref[home, 0])
            out_ref[home, 1] = jnp.where(here, facs[slot][:, 128:], out_ref[home, 1])
        return carry

    lax.fori_loop(0, (count + slots - 1) // slots, batch, 0)


def run_pick(pivot_owner, pivot_local, feat_t, prev):
    pivots = pivot_owner.size
    return pl.pallas_call(
        pick_kernel,
        out_shape=jax.ShapeDtypeStruct((16, 2, 8, 256), F32),
        in_specs=[HBM, HBM, HBM, HBM],
        out_specs=VMEM,
        scratch_shapes=[
            pltpu.SMEM(pivot_owner.shape, jnp.int32),
            pltpu.SMEM(pivot_local.shape, jnp.int32),
            pltpu.VMEM((8, feat_t.shape[0], 128), F32),
            pltpu.VMEM((8, 8, prev.shape[1]), F32),
            pltpu.SMEM((pivots + 1,), jnp.int32),
            pltpu.SemaphoreType.DMA((2,)),
            pltpu.SemaphoreType.DMA((2, 8)),
        ],
        compiler_params=pltpu.CompilerParams(vmem_limit_bytes=64 * 1024 * 1024),
        name="pick",
    )(pivot_owner, pivot_local, feat_t, prev)


def split2(value):
    high = value.astype(BF16)
    return high, (value - high.astype(F32)).astype(BF16)


def split3(value):
    high = value.astype(BF16)
    rest = value - high.astype(F32)
    mid = rest.astype(BF16)
    return high, mid, (rest - mid.astype(F32)).astype(BF16)


def factor_steps(block, result):
    size = block.shape[0]
    count = size // 8
    rows = [block[8 * at : 8 * at + 8] for at in range(count)]
    lane = lax.broadcasted_iota(jnp.int32, (8, size), 1)
    sub = lax.broadcasted_iota(jnp.int32, (8, size), 0)

    def spread(value, row):
        return jnp.broadcast_to(value[row : row + 1], (8, size))

    for home in range(count):
        first = 8 * home
        columns = [
            [jnp.broadcast_to(rows[at][:, first + k : first + k + 1], (8, size)) for at in range(home, count)]
            for k in range(8)
        ]
        inside = (lane >= first) & (lane < first + 8)
        top = jnp.where(inside, 0.0, rows[home])
        factors, pivots, diag = [], [], None
        for step in range(8):
            pivot = spread(columns[step][0], step)
            diag = pivot if diag is None else jnp.where(sub == step, pivot, diag)
            inverse = 1.0 / pivot
            factor = [value * inverse for value in columns[step]]
            factor[0] = jnp.where(sub > step, factor[0], 0.0)
            row = jnp.where(lane == first + step, 1.0, spread(top, step))
            if step < 7:
                top = top - factor[0] * row
                for k in range(step + 1, 8):
                    ahead = spread(columns[k][0], step)
                    columns[k] = [value - part * ahead for value, part in zip(columns[k], factor)]
            factors.append(factor)
            pivots.append(row)
        for at in range(home + 1, count):
            value = jnp.where(inside, 0.0, rows[at])
            for step in range(8):
                value = value - factors[step][at - home] * pivots[step]
            rows[at] = value
        unit = jnp.where(lane < sub + first, top, 0.0) + jnp.where(lane == sub + first, 1.0, 0.0)
        result.append(unit * lax.rsqrt(diag))
        yield


def stacked(value):
    high, low = split2(value)
    return jnp.concatenate(
        [jnp.concatenate([high, high], axis=1), jnp.concatenate([low, low], axis=1)], axis=0
    )


def panel_kernel(
    me_ref, noise_ref, owner_ref, place_ref, scales_ref, pivots_ref, feat_hbm, prev_hbm,
    new_hbm, resid_ref, part_ref,
    feat_ref, prev_ref, cols_ref, squares_ref, in_sems, out_sems, *, tile, chunk,
):
    feat, points = feat_ref.shape
    width = prev_ref.shape[1]
    size = owner_ref.shape[1]
    chunks = points // chunk
    noise = noise_ref[0]

    def incoming(at):
        here = pl.ds(at * chunk, chunk)
        return (
            pltpu.make_async_copy(feat_hbm.at[:, here], feat_ref.at[:, here], in_sems.at[0, at]),
            pltpu.make_async_copy(prev_hbm.at[here, :], prev_ref.at[here, :], in_sems.at[1, at]),
        )

    def outgoing(at):
        here = pl.ds(at * chunk, chunk)
        return pltpu.make_async_copy(cols_ref.at[here, :], new_hbm.at[here, :], out_sems.at[at])

    for at in range(chunks):
        for copy in incoming(at):
            copy.start()

    scales_row = scales_ref[...]
    scales_col = jnp.broadcast_to(scales_row, (8, feat)).T[:, :1]
    low = pivots_ref[:, 0].reshape(size, 256)
    piv_x = low[:, :feat]
    piv_f = jnp.concatenate([low[:, 128:], pivots_ref[:, 1].reshape(size, 256)], axis=1)
    piv_s = piv_x * scales_row
    piv_sq = jnp.sum(piv_s * piv_x, axis=1, keepdims=True)
    pad = jnp.zeros((size, 128 - feat), F32)
    lane = lax.broadcasted_iota(jnp.int32, (size, 128), 1)
    piv_left = jnp.concatenate([piv_x, pad], axis=1)
    piv_left = jnp.where(lane == feat, piv_sq, jnp.where(lane == feat + 1, 1.0, piv_left))
    piv_right = jnp.concatenate([piv_s, pad], axis=1)
    piv_right = jnp.where(lane == feat, -0.5, jnp.where(lane == feat + 1, -0.5 * piv_sq, piv_right))

    row_id = lax.broadcasted_iota(jnp.int32, (size, size), 0)
    col_id = lax.broadcasted_iota(jnp.int32, (size, size), 1)
    block = lax.dot_general(piv_left, piv_right, NT, precision=HIGH, preferred_element_type=F32)
    block = jnp.exp(block) + jnp.where(row_id == col_id, noise, 0.0)
    block = block - lax.dot_general(piv_f, piv_f, NT, precision=HIGH, preferred_element_type=F32)
    inverse_rows = []
    steps = factor_steps(block, inverse_rows)

    mine = jnp.where(owner_ref[...] == me_ref[0], place_ref[...], -1)
    fac_rhs = stacked(piv_f)
    x_high, x_mid, x_low = split3(piv_right)
    x_rhs = jnp.concatenate(
        [jnp.concatenate([x_high, x_high], axis=1), jnp.concatenate([x_mid, x_mid], axis=1)], axis=0
    )
    x_rest = jnp.concatenate([x_low, x_high], axis=1)
    sub = lax.broadcasted_iota(jnp.int32, (8, tile), 0)

    def columns(base):
        here = pl.ds(base, tile)
        xt = feat_ref[:, here]
        length = jnp.sum(xt * xt * scales_col, axis=0, keepdims=True)
        extra = jnp.where(sub == 0, length, jnp.where(sub == 1, 1.0, 0.0))
        left = jnp.concatenate([xt, extra, jnp.zeros((128 - feat - 8, tile), F32)], axis=0).T
        high, mid, low_part = split3(left)
        two = lax.dot_general(jnp.concatenate([high, mid], axis=1), x_rhs, NT, preferred_element_type=F32)
        rest = lax.dot_general(jnp.concatenate([high, low_part], axis=1), x_rest, NT, preferred_element_type=F32)
        kern = jnp.exp(two[:, :size] + (two[:, size:] + rest))
        ids = lax.broadcasted_iota(jnp.int32, (tile, size), 0) + base
        kern = kern + jnp.where(ids == mine, noise, 0.0)
        fac = prev_ref[here, :]
        high, low_part = split2(fac)
        both = lax.dot_general(
            jnp.concatenate([high, low_part], axis=1), fac_rhs, NT, preferred_element_type=F32
        )
        cols_ref[here, :] = kern - (both[:, :size] + both[:, size:])
        total = fac[:, :128] * fac[:, :128]
        for start in range(128, width, 128):
            total = total + fac[:, start : start + 128] * fac[:, start : start + 128]
        squares_ref[here, :] = total

    per_chunk = (size // 8) // chunks
    for at in range(chunks):
        for copy in incoming(at):
            copy.wait()
        for inner in range(chunk // tile):
            for _ in range(per_chunk * tile // chunk):
                next(steps)
            columns(at * chunk + inner * tile)
    for _ in steps:
        pass

    inv_rhs = stacked(jnp.concatenate(inverse_rows, axis=0))
    total = jnp.zeros((1, 128), F32)
    for at in range(chunks):
        for inner in range(chunk // tile):
            base = at * chunk + inner * tile
            here = pl.ds(base, tile)
            high, low_part = split2(cols_ref[here, :])
            both = lax.dot_general(
                jnp.concatenate([high, low_part], axis=1), inv_rhs, NT, preferred_element_type=F32
            )
            new = both[:, :size] + both[:, size:]
            cols_ref[here, :] = new
            gone = squares_ref[here, :] + new * new
            for sub_at in range(tile // 128):
                flipped = gone[sub_at * 128 : (sub_at + 1) * 128, :].T
                row = 1.0 + noise - jnp.sum(flipped, axis=0, keepdims=True)
                resid_ref[pl.ds(base // 128 + sub_at, 1), :] = row
                total = total + row
        outgoing(at).start()
    part_ref[...] = jnp.broadcast_to(jnp.sum(total, axis=1, keepdims=True), part_ref.shape)
    for at in range(chunks):
        outgoing(at).wait()


def run_panel(devices, me, noise, owner, place, scales, pivots, feat_t, prev):
    feat, points = feat_t.shape
    width = prev.shape[1]
    size = owner.shape[1]
    chunk = 512
    return pl.pallas_call(
        functools.partial(panel_kernel, tile=256, chunk=chunk),
        out_shape=(
            jax.ShapeDtypeStruct((points, size), F32),
            jax.ShapeDtypeStruct((points // 128, 128), F32),
            jax.ShapeDtypeStruct((devices, 128), F32),
        ),
        in_specs=[SMEM, SMEM, VMEM, VMEM, VMEM, VMEM, ANY, ANY],
        out_specs=(ANY, VMEM, VMEM),
        scratch_shapes=[
            pltpu.VMEM((feat, points), F32),
            pltpu.VMEM((points, width), F32),
            pltpu.VMEM((points, size), F32),
            pltpu.VMEM((points, 128), F32),
            pltpu.SemaphoreType.DMA((2, points // chunk)),
            pltpu.SemaphoreType.DMA((points // chunk,)),
        ],
        compiler_params=pltpu.CompilerParams(vmem_limit_bytes=64 * 1024 * 1024),
        name="panel",
    )(me, noise, owner, place, scales, pivots, feat_t, prev)


def local(devices, features, prev_factors, inv_scales, noise, pivot_owner, pivot_local):
    points, feat = features.shape
    pivots = pivot_owner.size
    feat_t = features.T
    me = lax.axis_index("rows").astype(jnp.int32).reshape(1)
    layer = groups_of(devices, ((1, 2), (16, 16)))
    column = groups_of(devices, ((2, 8),))

    picked = run_pick(pivot_owner, pivot_local, feat_t, prev_factors)
    part = exchange(picked.reshape(32, 8, 256), layer).sum(0)
    part = exchange(jnp.broadcast_to(part[None], (8, 8, 256)), column).sum(0)
    rows = exchange(jnp.broadcast_to(part[None], (32, 8, 256)), layer)
    new_factors, resid, part = run_panel(
        devices, me, noise, pivot_owner.reshape(1, pivots), pivot_local.reshape(1, pivots),
        inv_scales.reshape(1, feat), rows.reshape(16, 2, 8, 256), feat_t, prev_factors,
    )
    sums = exchange(part.reshape(devices, 1, 128), None)
    trace = jnp.sum(sums[:, 0, 0]).reshape(1)
    return new_factors, resid.reshape(points), trace


def solution(mesh):
    placed = (P("rows", None), P("rows", None), P(), P(), P(), P())
    return jax.shard_map(
        functools.partial(local, mesh.shape["rows"]),
        mesh=mesh,
        in_specs=placed,
        out_specs=(P("rows", None), P("rows"), P()),
        check_vma=False,
    )
```

time: 660 us -> 83.1 us (0.13)
  waiting for transfers between devices: 471 us -> 5.88 us
  matrix products: 56.7 us -> 0 us
  other arithmetic: 33.3 us -> 0.91 us
  blocking collectives: 75.9 us -> 51.5 us
  Pallas kernels: 0 us -> 14.1 us
  between operations: 15.2 us -> 1.33 us
    psum x2 -> x0, waiting for transfers between devices: 471 us -> none  [local(): lax.psum(select_rows(table, [features, prev_factors] + blocks), 'rows')]
    psum x1 -> x0, blocking collectives: 75.9 us -> none  [local(): trace = lax.psum(jnp.sum(residual_diag), 'rows').reshape(1)]
    dot_general x15 -> x0, matrix products: 52.1 us -> none  [the longest x2 16.6 us: local(): jnp.dot(prev_factors, piv_fac[:, :prev_width].T, precision=HIGH, preferre...]
    all_to_all x0 -> x3, blocking collectives: none -> 51.5 us  [exchange(): lax.all_to_all(blocks, 'rows', 0, 0, axis_index_groups=groups, tiled=True)]
    another operation x10 -> x0, other arithmetic: 24.1 us -> none  [the longest x6 13 us: local(): lower = jnp.linalg.cholesky(pivot_block)]
    pallas_call x0 -> x2, Pallas kernels: none -> 14.1 us  [the longest x1 10.9 us: run_panel(): pl.pallas_call(functools.partial(panel_kernel, tile=256, chunk=chunk), ou...]
  transfers between devices with their start and end apart: 2 -> 1, of which waited for: 2 -> 1; matrix products, arithmetic and copies ran while one was open for 2% -> 3% of each run, Pallas kernels for 0% -> 0%
where the time goes in v2:
time: 83.1 us; the launch traced here: 83 us
  blocking collectives  51.5 us (62%)
  Pallas kernels  14.1 us (17%)
  waiting for transfers between devices  5.88 us (7%)
  starting transfers between devices  5.84 us (7%)
  local copies, waits for them, and re-layouts  3.34 us (4%)
  between operations  1.33 us (2%)
  other arithmetic  0.91 us (1%)
    all_to_all x3, blocking collectives, exchange(): lax.all_to_all(blocks, 'rows', 0, 0, axis_index_groups=groups, tiled=True)  51.5 us
    pallas_call x1, Pallas kernels, run_panel(): pl.pallas_call(functools.partial(panel_kernel, tile=256, chunk=chunk), ou...  10.9 us
    all_to_all x1, waiting for transfers between devices, exchange(): lax.all_to_all(blocks, 'rows', 0, 0, axis_index_groups=groups, tiled=True)  5.88 us
    all_to_all x1, starting transfers between devices, exchange(): lax.all_to_all(blocks, 'rows', 0, 0, axis_index_groups=groups, tiled=True)  5.84 us
    pallas_call x1, Pallas kernels, run_pick(): pl.pallas_call(pick_kernel, out_shape=jax.ShapeDtypeStruct((16, 2, 8, 256...  3.25 us
  transfers between devices with their start and end apart: 1, of which 1 were waited for; matrix products, arithmetic and copies ran while one was open for 3% of the time, Pallas kernels for 0%

profile of v2, /device:TPU:1, one launch (start us, length us, event | category | flops | bytes accessed | tf_op | source)
XLA Modules:
  0.0 83.0 jit_solution(17270742043617338604)
XLA Ops:
  0.6 3.3 %pick.1 = f32[16,2,8,256]{3,2,1,0:T(8,128)} custom-call(s32[2,64]{1,0:T(2,128)} %owner_hbm.1, s32[2,64]{1,0:T(2,128)} %place_hbm.1, f32[64,4096]{1,0:T(8,128)} %bitcast.10, f32[4096,384]{1,0:T(8,128)} %prev_hbm.3), custom_call_target="tpu_custom_call" | custom-call | tf_op jit(solution)/shard_map/pick/pallas_call | solution.py:112
  3.9 17.6 %all_to_all.20 = f32[32,8,256]{2,1,0:T(8,128)S(1)} all-to-all(f32[32,8,256]{2,1,0:T(8,128)} %bitcast.12), channel_id=1, replica_groups={{0,1,16,17,32,33,48,49,64,65,80,81,96,97,112,113,128,129,144,145,160,16..., dimensions={0} | all-to-all | bytes 524288 | tf_op jit(solution)/shard_map/all_to_all | solution.py:31
  21.5 15.2 %all_to_all.21 = f32[8,8,256]{2,1,0:T(8,128)S(1)} all-to-all(f32[8,8,256]{2,1,0:T(8,128)S(1)} %broadcast_in_dim.4), channel_id=1, replica_groups={{0,2,4,6,8,10,12,14},{1,3,5,7,9,11,13,15},{16,18,20,22,24,26,28,30},{17..., dimensions={0} | all-to-all | bytes 131072 | tf_op jit(solution)/shard_map/all_to_all | solution.py:31
  36.7 0.7 broadcast_in_dim.5
  37.4 5.8 %all-to-all-start.2 = ((f32[32,8,256]{2,1,0:T(8,128)}), f32[32,8,256]{2,1,0:T(8,128)}, u32[]{:S(2)}, u32[]{:S(2)}) async-start(f32[32,8,256]{2,1,0:T(8,128)} %broadcast_in_dim.5), calls=%async_computation.2 | async-start | bytes 524288 | tf_op jit(solution)/shard_map/all_to_all | solution.py:31
  43.2 1.3 %reshape.36.owner_ref = s32[1,128]{1,0:T(1,128)} reshape(s32[2,64]{1,0:T(2,128)} %owner_hbm.1) | data formatting | bytes 1024 | tf_op jit(solution)/shard_map/reshape | solution.py:348
  44.6 1.3 %reshape.37.place_ref = s32[1,128]{1,0:T(1,128)} reshape(s32[2,64]{1,0:T(2,128)} %place_hbm.1) | data formatting | bytes 1024 | tf_op jit(solution)/shard_map/reshape | solution.py:348
  46.5 5.9 %all-to-all-done.2 = f32[32,8,256]{2,1,0:T(8,128)} async-done(((f32[32,8,256]{2,1,0:T(8,128)}), f32[32,8,256]{2,1,0:T(8,128)}, u32[]{:S(2)}, u32[]{:S(2)}) %all-to-all-start.2) | async-done | bytes 262176 | tf_op jit(solution)/shard_map/all_to_all | solution.py:31
  52.4 10.9 %panel.1 = (f32[4096,128]{1,0:T(8,128)}, f32[32,128]{1,0:T(8,128)}, f32[256,128]{1,0:T(8,128)}) custom-call(s32[1]{0:T(128)} %bitcast.me_ref, f32[1]{0:T(128)S(6)} %copy.11.noise_ref, s32[1,128]{1,0:T(1,128)} %reshape.36.owner_ref, s32[1,128]{1,0:T(1,128)} %reshape.37.place_ref, f32[1,64]{1,0:T(1,128)} %bitcast.14, f32[16,2,8,256]{3,2,1,0:T(8,128)} %bitcast.4.pivots_ref, ...), custom_call_target="tpu_custom_call" | custom-call | tf_op jit(solution)/shard_map/panel/pallas_call | solution.py:313
  63.3 18.8 %all_to_all.22 = f32[256,1,128]{2,1,0:T(1,128)S(1)} all-to-all(f32[256,1,128]{2,1,0:T(1,128)} %bitcast.13), channel_id=1, replica_groups=mesh['rows'=256] {'rows'}, dimensions={0} | all-to-all | bytes 262144 | tf_op jit(solution)/shard_map/all_to_all | solution.py:31
  82.1 0.9 %slice_reduce_fusion = f32[]{:T(128)} fusion(f32[256,1,128]{2,1,0:T(1,128)S(1)} %all_to_all.22), kind=kLoop, calls=%fused_computation | loop fusion | flops 255 | bytes 1028 | tf_op jit(solution)/shard_map/reduce_sum | solution.py:352
  (3 shorter events, 0.1 us)
Async XLA Ops:
  37.4 15.0 %all-to-all-start.2 = ((f32[32,8,256]{2,1,0:T(8,128)}), f32[32,8,256]{2,1,0:T(8,128)}, u32[]{:S(2)}, u32[]{:S(2)}) async-start(f32[32,8,256]{2,1,0:T(8,128)} %broadcast_in_dim.5), calls=%async_computation.2 | async-start | bytes 524288 | tf_op jit(solution)/shard_map/all_to_all | solution.py:31

commit v3 on v2

--- a/solution.py
+++ b/solution.py
@@ -15,6 +15,11 @@
 ANY = pl.BlockSpec(memory_space=pl.ANY)
 HBM = pl.BlockSpec(memory_space=pltpu.HBM)
 NT = (((1,), (1,)), ((), ()))
+SMALL = 16 * 1024 * 1024
+LAYERS = 8
+RANKS = 8
+SPOTS = 32
+SPLITS = 4
 
 
 def groups_of(total, fields):
@@ -32,8 +37,8 @@
 
 
 def pick_kernel(
-    owner_hbm, place_hbm, feat_hbm, prev_hbm, out_ref, owner_ref, place_ref, feat_part, prev_part, found,
-    table_sems, sems,
+    round_ref, owner_hbm, place_hbm, feat_hbm, prev_hbm, out_ref, owner_ref, place_ref, feat_part, prev_part,
+    found, table_sems, sems,
 ):
     tables = (
         pltpu.make_async_copy(owner_hbm, owner_ref, table_sems.at[0]),
@@ -41,91 +46,189 @@
     )
     for copy in tables:
         copy.start()
-    out_ref[...] = jnp.zeros_like(out_ref)
     feat_part[...] = jnp.zeros_like(feat_part)
     panels, panel = owner_ref.shape
     feat = feat_hbm.shape[0]
-    slots = feat_part.shape[0]
     me = lax.axis_index("rows")
+    first = (round_ref[0] // SPLITS) * RANKS
     for copy in tables:
         copy.wait()
     count = jnp.int32(0)
     for pivot in range(panels * panel):
         found[count] = pivot
         count = count + (owner_ref[pivot // panel, pivot % panel] == me).astype(jnp.int32)
+    count = jnp.clip(count - first, 0, RANKS)
 
     def place_of(at):
-        pivot = found[at]
-        return pivot, place_ref[pivot // panel, lax.rem(pivot, panel)]
-
-    def copies(at, place):
+        pivot = found[first + at]
+        return place_ref[pivot // panel, lax.rem(pivot, panel)]
+
+    def copies(at):
+        place = place_of(at)
         wide = pl.ds(pl.multiple_of((place // 128) * 128, 128), 128)
         rows = pl.ds(pl.multiple_of((place // 8) * 8, 8), 8)
-        slot = lax.rem(at, slots)
         return (
-            pltpu.make_async_copy(feat_hbm.at[:, wide], feat_part.at[slot], sems.at[0, slot]),
-            pltpu.make_async_copy(prev_hbm.at[rows, :], prev_part.at[slot], sems.at[1, slot]),
+            pltpu.make_async_copy(feat_hbm.at[:, wide], feat_part.at[at], sems.at[0, at]),
+            pltpu.make_async_copy(prev_hbm.at[rows, :], prev_part.at[at], sems.at[1, at]),
         )
 
     def start(at, carry):
-        for copy in copies(at, place_of(at)[1]):
+        for copy in copies(at):
             copy.start()
         return carry
 
     def land(at, carry):
-        for copy in copies(at, place_of(at)[1]):
+        for copy in copies(at):
             copy.wait()
         return carry
 
-    sub = lax.broadcasted_iota(jnp.int32, (8, 128), 0)
-    lane = lax.broadcasted_iota(jnp.int32, (8, 128), 1)
-    wide_sub = lax.broadcasted_iota(jnp.int32, (8, 256), 0)
-    fac_sub = lax.broadcasted_iota(jnp.int32, prev_part.shape[1:], 0)
-
-    def batch(at, carry):
-        first = at * slots
-        last = jnp.minimum(first + slots, count)
-        lax.fori_loop(first, last, start, 0)
-        lax.fori_loop(first, last, land, 0)
-        homes, xs, facs = [], 0.0, []
-        for slot in range(slots):
-            used = first + slot < last
-            pivot, place = place_of(jnp.where(used, first + slot, first))
-            homes.append((pivot // 8, jnp.where(used, lax.rem(pivot, 8), -1)))
-            only = jnp.where((sub == slot) & (lane == lax.rem(place, 128)), 1.0, 0.0)
-            xs = xs + lax.dot_general(only, feat_part[slot], NT, precision=HIGH, preferred_element_type=F32)
-            fac = jnp.where(fac_sub == lax.rem(place, 8), prev_part[slot], 0.0)
+    lax.fori_loop(0, count, start, 0)
+    lax.fori_loop(0, count, land, 0)
+
+    @pl.when(count > 0)
+    def _():
+        sub = lax.broadcasted_iota(jnp.int32, (RANKS, 128), 0)
+        lane = lax.broadcasted_iota(jnp.int32, (RANKS, 128), 1)
+        fac_sub = lax.broadcasted_iota(jnp.int32, prev_part.shape[1:], 0)
+        xs, facs = 0.0, []
+        for at in range(RANKS):
+            used = at < count
+            place = place_of(jnp.where(used, at, 0))
+            only = jnp.where((sub == at) & (lane == lax.rem(place, 128)) & used, 1.0, 0.0)
+            xs = xs + lax.dot_general(only, feat_part[at], NT, precision=HIGH, preferred_element_type=F32)
+            fac = jnp.where((fac_sub == lax.rem(place, 8)) & used, prev_part[at], 0.0)
             facs.append(jnp.sum(fac, axis=0, keepdims=True))
-        xs = jnp.concatenate([xs, jnp.zeros((slots, 128 - feat), F32)], axis=1)
-        for slot, (home, inner) in enumerate(homes):
-            here = wide_sub == inner
-            left = jnp.concatenate([xs[slot : slot + 1], facs[slot][:, :128]], axis=1)
-            out_ref[home, 0] = jnp.where(here, left, out_ref[home, 0])
-            out_ref[home, 1] = jnp.where(here, facs[slot][:, 128:], out_ref[home, 1])
-        return carry
-
-    lax.fori_loop(0, (count + slots - 1) // slots, batch, 0)
-
-
-def run_pick(pivot_owner, pivot_local, feat_t, prev):
-    pivots = pivot_owner.size
+        facs = jnp.concatenate(facs, axis=0)
+        pad = jnp.zeros((RANKS, 128 - feat), F32)
+        halves = (jnp.concatenate([xs, pad, facs[:, :128]], axis=1), facs[:, 128:])
+        for at in range(out_ref.shape[0]):
+            for half in range(2):
+                out_ref[at, half] = halves[half]
+
+    @pl.when(count == 0)
+    def _():
+        out_ref[...] = jnp.zeros_like(out_ref)
+
+
+def run_pick(at_round, pivot_owner, pivot_local, feat_t, prev):
     return pl.pallas_call(
         pick_kernel,
-        out_shape=jax.ShapeDtypeStruct((16, 2, 8, 256), F32),
-        in_specs=[HBM, HBM, HBM, HBM],
+        out_shape=jax.ShapeDtypeStruct((16, 2, RANKS, 256), F32),
+        in_specs=[SMEM, HBM, HBM, HBM, HBM],
         out_specs=VMEM,
         scratch_shapes=[
             pltpu.SMEM(pivot_owner.shape, jnp.int32),
             pltpu.SMEM(pivot_local.shape, jnp.int32),
-            pltpu.VMEM((8, feat_t.shape[0], 128), F32),
-            pltpu.VMEM((8, 8, prev.shape[1]), F32),
-            pltpu.SMEM((pivots + 1,), jnp.int32),
+            pltpu.VMEM((RANKS, feat_t.shape[0], 128), F32),
+            pltpu.VMEM((RANKS, 8, prev.shape[1]), F32),
+            pltpu.SMEM((pivot_owner.size + 1,), jnp.int32),
             pltpu.SemaphoreType.DMA((2,)),
-            pltpu.SemaphoreType.DMA((2, 8)),
+            pltpu.SemaphoreType.DMA((2, RANKS)),
         ],
         compiler_params=pltpu.CompilerParams(vmem_limit_bytes=64 * 1024 * 1024),
         name="pick",
-    )(pivot_owner, pivot_local, feat_t, prev)
+    )(at_round, pivot_owner, pivot_local, feat_t, prev)
+
+
+def table_kernel(
+    round_ref, noise_ref, owner_ref, place_ref, scales_ref, pack_ref, pivots_ref, aux_ref, more_ref, rounds_ref
+):
+    panels, panel = owner_ref.shape
+    size = panels * panel
+    at_round = round_ref[0]
+    window_now = (at_round // SPLITS).astype(F32)
+    split_now = lax.rem(at_round, SPLITS).astype(F32)
+    layer_now = lax.rem(lax.axis_index("rows") // 2, LAYERS).astype(F32)
+    owner_row = jnp.concatenate([owner_ref[at : at + 1, :] for at in range(panels)], axis=1).astype(F32)
+    place_row = jnp.concatenate([place_ref[at : at + 1, :] for at in range(panels)], axis=1).astype(F32)
+    mine = jnp.where(owner_row == lax.axis_index("rows").astype(F32), place_row, -1.0)
+    scales = jnp.concatenate([scales_ref[...], jnp.zeros_like(scales_ref)], axis=1)
+    sub = lax.broadcasted_iota(jnp.int32, aux_ref.shape, 0)
+    aux_ref[...] = jnp.where(sub == 0, mine, jnp.where(sub == 1, scales, noise_ref[0]))
+    more_ref[...] = jnp.zeros_like(more_ref)
+    owner_row = jnp.broadcast_to(owner_row, (size, size))
+    owner_col = owner_row.T
+    row_id = lax.broadcasted_iota(jnp.int32, (size, size), 0)
+    col_id = lax.broadcasted_iota(jnp.int32, (size, size), 1)
+    earlier = col_id < row_id
+
+    def whole(value, unit):
+        return jnp.floor(value * (1.0 / unit))
+
+    def rest(value, unit):
+        return value - unit * whole(value, unit)
+
+    def ranks(same):
+        found = jnp.sum(jnp.where(same & earlier, 1.0, 0.0), axis=1, keepdims=True)
+        return jnp.broadcast_to(found, (size, size))
+
+    rank = ranks(owner_row == owner_col)
+    window = whole(rank, RANKS)
+    layer_row = rest(whole(owner_row, 2), LAYERS)
+    layer_col = rest(whole(owner_col, 2), LAYERS)
+    spot = ranks((layer_row == layer_col) & (window == window.T))
+    split = whole(spot, SPOTS)
+    spot = rest(spot, SPOTS)
+    active = (window == window_now) & (split == split_now)
+    rounds_ref[0] = jnp.max(window * SPLITS + split).astype(jnp.int32) + 1
+
+    wide = lax.broadcasted_iota(jnp.int32, (size, LAYERS * SPOTS), 1).astype(F32)
+    both = lambda value: jnp.concatenate([value, value], axis=1)
+    goal = both(jnp.where(active, layer_col * SPOTS + spot, -1.0))
+    pivots_ref[...] = jnp.where(wide == goal, 1.0, 0.0)
+    origin = (whole(owner_col, 2 * LAYERS) * 2 + rest(owner_col, 2)) * RANKS + rest(rank, RANKS)
+    origin = jnp.where(wide == both(origin), 1.0, 0.0).astype(BF16)
+    spot_row = jnp.where(active & (layer_col == layer_now), spot, -1.0).T[:SPOTS]
+    target = lax.broadcasted_iota(jnp.int32, (SPOTS, size), 0).astype(F32)
+    target = jnp.where(spot_row == target, 1.0, 0.0).astype(BF16)
+    pack_ref[...] = jnp.dot(target, origin, preferred_element_type=F32)
+
+
+def run_table(at_round, noise, pivot_owner, pivot_local, scales):
+    size = pivot_owner.size
+    return pl.pallas_call(
+        table_kernel,
+        out_shape=(
+            jax.ShapeDtypeStruct((SPOTS, 32 * RANKS), F32),
+            jax.ShapeDtypeStruct((size, LAYERS * SPOTS), F32),
+            jax.ShapeDtypeStruct((8, size), F32),
+            jax.ShapeDtypeStruct((size, 512), F32),
+            jax.ShapeDtypeStruct((1,), jnp.int32),
+        ),
+        in_specs=[SMEM, SMEM, VMEM, VMEM, VMEM],
+        out_specs=(VMEM, VMEM, VMEM, VMEM, SMEM),
+        compiler_params=pltpu.CompilerParams(vmem_limit_bytes=SMALL),
+        name="table",
+    )(at_round, noise, pivot_owner, pivot_local, scales)
+
+
+def pack_kernel(table_ref, rows_ref, out_ref):
+    packed = jnp.dot(table_ref[...], rows_ref[...], precision=HIGH, preferred_element_type=F32)
+    for at in range(out_ref.shape[0]):
+        out_ref[at] = packed
+
+
+def run_pack(table, rows):
+    return pl.pallas_call(
+        pack_kernel,
+        out_shape=jax.ShapeDtypeStruct((LAYERS, SPOTS, 256), F32),
+        in_specs=[VMEM, VMEM],
+        out_specs=VMEM,
+        compiler_params=pltpu.CompilerParams(vmem_limit_bytes=SMALL),
+        name="pack",
+    )(table, rows)
+
+
+def unpack(table, near, far, core):
+    first = jnp.where(core == 0, near, far).reshape(LAYERS * SPOTS, 256)
+    second = jnp.where(core == 0, far, near).reshape(LAYERS * SPOTS, 256)
+    return jnp.concatenate(
+        [
+            jnp.dot(table, first, precision=HIGH, preferred_element_type=F32),
+            jnp.dot(table, second, precision=HIGH, preferred_element_type=F32),
+        ],
+        axis=1,
+    )
 
 
 def split2(value):
@@ -191,15 +294,22 @@
 
 
 def panel_kernel(
-    me_ref, noise_ref, owner_ref, place_ref, scales_ref, pivots_ref, feat_hbm, prev_hbm,
+    rounds_ref, aux_hbm, table_hbm, near_hbm, far_hbm, more_hbm, feat_hbm, prev_hbm,
     new_hbm, resid_ref, part_ref,
-    feat_ref, prev_ref, cols_ref, squares_ref, in_sems, out_sems, *, tile, chunk,
+    aux_ref, table_ref, near_ref, far_ref, more_ref, feat_ref, prev_ref, cols_ref, squares_ref,
+    first_sems, in_sems, out_sems, *, tile, chunk,
 ):
     feat, points = feat_ref.shape
     width = prev_ref.shape[1]
-    size = owner_ref.shape[1]
+    size = aux_ref.shape[1]
     chunks = points // chunk
-    noise = noise_ref[0]
+
+    pairs = ((near_hbm, near_ref), (far_hbm, far_ref), (table_hbm, table_ref), (aux_hbm, aux_ref))
+    first_copies = [
+        pltpu.make_async_copy(source, target, first_sems.at[at]) for at, (source, target) in enumerate(pairs)
+    ]
+    for copy in first_copies:
+        copy.start()
 
     def incoming(at):
         here = pl.ds(at * chunk, chunk)
@@ -212,15 +322,30 @@
         here = pl.ds(at * chunk, chunk)
         return pltpu.make_async_copy(cols_ref.at[here, :], new_hbm.at[here, :], out_sems.at[at])
 
+    @pl.when(rounds_ref[0] > 1)
+    def _():
+        copy = pltpu.make_async_copy(more_hbm, more_ref, first_sems.at[len(pairs)])
+        copy.start()
+        copy.wait()
+
+    @pl.when(rounds_ref[0] <= 1)
+    def _():
+        more_ref[...] = jnp.zeros_like(more_ref)
+
+    for copy in first_copies:
+        copy.wait()
     for at in range(chunks):
         for copy in incoming(at):
             copy.start()
 
-    scales_row = scales_ref[...]
-    scales_col = jnp.broadcast_to(scales_row, (8, feat)).T[:, :1]
-    low = pivots_ref[:, 0].reshape(size, 256)
-    piv_x = low[:, :feat]
-    piv_f = jnp.concatenate([low[:, 128:], pivots_ref[:, 1].reshape(size, 256)], axis=1)
+    mine = aux_ref[0:1, :]
+    scales_row = aux_ref[1:2, :feat]
+    noise = aux_ref[2:3, :]
+    scales_col = jnp.broadcast_to(aux_ref[1:2, :], (8, size)).T[:feat, :1]
+    core = lax.rem(lax.axis_index("rows"), 2)
+    rows = unpack(table_ref[...], near_ref[...], far_ref[...], core) + more_ref[...]
+    piv_x = rows[:, :feat]
+    piv_f = rows[:, 128:]
     piv_s = piv_x * scales_row
     piv_sq = jnp.sum(piv_s * piv_x, axis=1, keepdims=True)
     pad = jnp.zeros((size, 128 - feat), F32)
@@ -238,7 +363,6 @@
     inverse_rows = []
     steps = factor_steps(block, inverse_rows)
 
-    mine = jnp.where(owner_ref[...] == me_ref[0], place_ref[...], -1)
     fac_rhs = stacked(piv_f)
     x_high, x_mid, x_low = split3(piv_right)
     x_rhs = jnp.concatenate(
@@ -246,6 +370,7 @@
     )
     x_rest = jnp.concatenate([x_low, x_high], axis=1)
     sub = lax.broadcasted_iota(jnp.int32, (8, tile), 0)
+    ids = lax.broadcasted_iota(jnp.int32, (tile, size), 0).astype(F32)
 
     def columns(base):
         here = pl.ds(base, tile)
@@ -257,8 +382,7 @@
         two = lax.dot_general(jnp.concatenate([high, mid], axis=1), x_rhs, NT, preferred_element_type=F32)
         rest = lax.dot_general(jnp.concatenate([high, low_part], axis=1), x_rest, NT, preferred_element_type=F32)
         kern = jnp.exp(two[:, :size] + (two[:, size:] + rest))
-        ids = lax.broadcasted_iota(jnp.int32, (tile, size), 0) + base
-        kern = kern + jnp.where(ids == mine, noise, 0.0)
+        kern = kern + jnp.where(ids == mine - base, noise, 0.0)
         fac = prev_ref[here, :]
         high, low_part = split2(fac)
         both = lax.dot_general(
@@ -305,10 +429,10 @@
         outgoing(at).wait()
 
 
-def run_panel(devices, me, noise, owner, place, scales, pivots, feat_t, prev):
+def run_panel(devices, rounds, aux, table, near, far, more, feat_t, prev):
     feat, points = feat_t.shape
     width = prev.shape[1]
-    size = owner.shape[1]
+    size = aux.shape[1]
     chunk = 512
     return pl.pallas_call(
         functools.partial(panel_kernel, tile=256, chunk=chunk),
@@ -317,37 +441,52 @@
             jax.ShapeDtypeStruct((points // 128, 128), F32),
             jax.ShapeDtypeStruct((devices, 128), F32),
         ),
-        in_specs=[SMEM, SMEM, VMEM, VMEM, VMEM, VMEM, ANY, ANY],
+        in_specs=[SMEM] + [ANY] * 7,
         out_specs=(ANY, VMEM, VMEM),
         scratch_shapes=[
+            pltpu.VMEM(aux.shape, F32),
+            pltpu.VMEM(table.shape, F32),
+            pltpu.VMEM(near.shape, F32),
+            pltpu.VMEM(far.shape, F32),
+            pltpu.VMEM(more.shape, F32),
             pltpu.VMEM((feat, points), F32),
             pltpu.VMEM((points, width), F32),
             pltpu.VMEM((points, size), F32),
             pltpu.VMEM((points, 128), F32),
+            pltpu.SemaphoreType.DMA((5,)),
             pltpu.SemaphoreType.DMA((2, points // chunk)),
             pltpu.SemaphoreType.DMA((points // chunk,)),
         ],
         compiler_params=pltpu.CompilerParams(vmem_limit_bytes=64 * 1024 * 1024),
         name="panel",
-    )(me, noise, owner, place, scales, pivots, feat_t, prev)
+    )(rounds, aux, table, near, far, more, feat_t, prev)
 
 
 def local(devices, features, prev_factors, inv_scales, noise, pivot_owner, pivot_local):
     points, feat = features.shape
-    pivots = pivot_owner.size
     feat_t = features.T
-    me = lax.axis_index("rows").astype(jnp.int32).reshape(1)
     layer = groups_of(devices, ((1, 2), (16, 16)))
-    column = groups_of(devices, ((2, 8),))
-
-    picked = run_pick(pivot_owner, pivot_local, feat_t, prev_factors)
-    part = exchange(picked.reshape(32, 8, 256), layer).sum(0)
-    part = exchange(jnp.broadcast_to(part[None], (8, 8, 256)), column).sum(0)
-    rows = exchange(jnp.broadcast_to(part[None], (32, 8, 256)), layer)
-    new_factors, resid, part = run_panel(
-        devices, me, noise, pivot_owner.reshape(1, pivots), pivot_local.reshape(1, pivots),
-        inv_scales.reshape(1, feat), rows.reshape(16, 2, 8, 256), feat_t, prev_factors,
-    )
+    column = groups_of(devices, ((2, LAYERS),))
+    cores = [(at, at ^ 1) for at in range(devices)]
+
+    def fetch(at_round):
+        picked = run_pick(at_round, pivot_owner, pivot_local, feat_t, prev_factors)
+        landed = exchange(picked.reshape(32, RANKS, 256), layer)
+        pack_table, table, aux, more, rounds = run_table(
+            at_round, noise, pivot_owner, pivot_local, inv_scales.reshape(1, feat)
+        )
+        packed = run_pack(pack_table, landed.reshape(32 * RANKS, 256))
+        near = exchange(packed, column)
+        return table, near, lax.ppermute(near, "rows", cores), aux, more, rounds
+
+    def again(carry):
+        at_round, more = carry
+        table, near, far, *_ = fetch(at_round.reshape(1))
+        return at_round + 1, more + unpack(table, near, far, lax.rem(lax.axis_index("rows"), 2))
+
+    table, near, far, aux, more, rounds = fetch(jnp.zeros((1,), jnp.int32))
+    _, more = lax.while_loop(lambda carry: carry[0] < rounds[0], again, (jnp.int32(1), more))
+    new_factors, resid, part = run_panel(devices, rounds, aux, table, near, far, more, feat_t, prev_factors)
     sums = exchange(part.reshape(devices, 1, 128), None)
     trace = jnp.sum(sums[:, 0, 0]).reshape(1)
     return new_factors, resid.reshape(points), trace

time: 83.1 us -> 76.2 us (0.917)
  blocking collectives: 51.5 us -> 18.9 us
  waiting for transfers between devices: 5.88 us -> 18.5 us
  starting transfers between devices: 5.84 us -> 17.2 us
  Pallas kernels: 14.1 us -> 17.6 us
  local copies, waits for them, and re-layouts: 3.34 us -> 1.23 us
    all_to_all x3 -> x1, blocking collectives: 51.5 us -> 18.9 us  [exchange(): lax.all_to_all(blocks, 'rows', 0, 0, axis_index_groups=groups, tiled=True)]
    all_to_all x1 -> x2, waiting for transfers between devices: 5.88 us -> 17.6 us  [exchange(): lax.all_to_all(blocks, 'rows', 0, 0, axis_index_groups=groups, tiled=True)]
    all_to_all x1 -> x2, starting transfers between devices: 5.84 us -> 16.6 us  [exchange(): lax.all_to_all(blocks, 'rows', 0, 0, axis_index_groups=groups, tiled=True)]
    pallas_call x1 -> x3, Pallas kernels: 3.25 us -> 5.95 us  [the longest x1 3.21 us: run_pick(): pl.pallas_call(pick_kernel, out_shape=jax.ShapeDtypeStruct((16, 2, RANKS,...]
    reshape x2 -> x0, local copies, waits for them, and re-layouts: 2.61 us -> none  [the longest x1 1.33 us: local(): pivot_owner.reshape(1, pivots)]
    unnamed x0 -> x4, local copies, waits for them, and re-layouts: none -> 1.23 us
    ppermute x0 -> x1, waiting for transfers between devices: none -> 0.84 us  [fetch(): return (table, near, lax.ppermute(near, 'rows', cores), aux, more, rounds)]
  transfers between devices with their start and end apart: 1 -> 3, of which waited for: 1 -> 3; matrix products, arithmetic and copies ran while one was open for 3% -> 0% of each run, Pallas kernels for 0% -> 2%
where the time goes in v3:
time: 76.2 us
  blocking collectives  18.9 us (25%)
  waiting for transfers between devices  18.5 us (24%)
  Pallas kernels  17.6 us (23%)
  starting transfers between devices  17.2 us (23%)
  between operations  1.33 us (2%)
  local copies, waits for them, and re-layouts  1.23 us (2%)
  other arithmetic  0.87 us (1%)
    all_to_all x1, blocking collectives, exchange(): lax.all_to_all(blocks, 'rows', 0, 0, axis_index_groups=groups, tiled=True)  18.9 us
    all_to_all x2, waiting for transfers between devices, exchange(): lax.all_to_all(blocks, 'rows', 0, 0, axis_index_groups=groups, tiled=True)  17.6 us
    all_to_all x2, starting transfers between devices, exchange(): lax.all_to_all(blocks, 'rows', 0, 0, axis_index_groups=groups, tiled=True)  16.6 us
    pallas_call x1, Pallas kernels, run_panel(): pl.pallas_call(functools.partial(panel_kernel, tile=256, chunk=chunk), ou...  11.6 us
    pallas_call x1, Pallas kernels, run_pick(): pl.pallas_call(pick_kernel, out_shape=jax.ShapeDtypeStruct((16, 2, RANKS,...  3.21 us
    pallas_call x1, Pallas kernels, run_table(): pl.pallas_call(table_kernel, out_shape=(jax.ShapeDtypeStruct((SPOTS, 32 *...  1.81 us
  transfers between devices with their start and end apart: 3, of which 3 were waited for; matrix products, arithmetic and copies ran while one was open for 0% of the time, Pallas kernels for 2%

profile of v3, /device:TPU:1, one launch (start us, length us, event | category | flops | bytes accessed | tf_op | source)
XLA Modules:
  0.0 76.2 jit_solution(18412211140798145852)
XLA Ops:
  0.6 3.2 %pick.2 = f32[16,2,8,256]{3,2,1,0:T(8,128)} custom-call(s32[1]{0:T(128)} %constant.3.clone.1.round_ref, s32[2,64]{1,0:T(2,128)} %owner_hbm.1, s32[2,64]{1,0:T(2,128)} %place_hbm.1, f32[64,4096]{1,0:T(8,128)} %bitcast.43, f32[4096,384]{1,0:T(8,128)} %prev_hbm.3), custom_call_target="tpu_custom_call" | custom-call | tf_op jit(solution)/shard_map/pick/pallas_call | solution.py:114
  3.8 7.3 %all-to-all-start.2 = ((f32[32,8,256]{2,1,0:T(8,128)}), f32[32,8,256]{2,1,0:T(8,128)S(1)}, u32[]{:S(2)}, u32[]{:S(2)}) async-start(f32[32,8,256]{2,1,0:T(8,128)} %bitcast.48), calls=%async_computation.2 | async-start | bytes 524288 | tf_op jit(solution)/shard_map/all_to_all | solution.py:36
  11.8 1.8 %table.2 = (f32[32,256]{1,0:T(8,128)S(1)}, f32[128,256]{1,0:T(8,128)S(1)}, f32[8,128]{1,0:T(8,128)S(1)}, f32[128,512]{1,0:T(8,128)}, s32[1]{0:T(128)}) custom-call(s32[1]{0:T(128)} %constant.3.clone.1.round_ref, f32[1]{0:T(128)S(6)} %copy.16.noise_ref, s32[2,64]{1,0:T(2,128)} %owner_hbm.1, s32[2,64]{1,0:T(2,128)} %place_hbm.1, f32[1,64]{1,0:T(1,128)} %bitcast.50), custom_call_target="tpu_custom_call" | custom-call | tf_op jit(solution)/shard_map/table/pallas_call | solution.py:189
  13.6 0.0 copy-start
  13.6 0.6 copy-done
  14.2 0.0 copy-start.1
  14.2 0.6 copy-done.1
  14.8 5.3 %all-to-all-done.2 = f32[32,8,256]{2,1,0:T(8,128)S(1)} async-done(((f32[32,8,256]{2,1,0:T(8,128)}), f32[32,8,256]{2,1,0:T(8,128)S(1)}, u32[]{:S(2)}, u32[]{:S(2)}) %all-to-all-start.2) | async-done | bytes 262176 | tf_op jit(solution)/shard_map/all_to_all | solution.py:36
  20.1 0.9 %pack.2 = f32[8,32,256]{2,1,0:T(8,128)} custom-call(f32[32,256]{1,0:T(8,128)S(1)} %get-tuple-element.64.table_ref, f32[256,256]{1,0:T(8,128)S(1)} %bitcast.42), custom_call_target="tpu_custom_call" | custom-call | tf_op jit(solution)/shard_map/pack/pallas_call | solution.py:212
  21.1 9.3 %all-to-all-start.3 = ((f32[8,32,256]{2,1,0:T(8,128)}), f32[8,32,256]{2,1,0:T(8,128)}, u32[]{:S(2)}, u32[]{:S(2)}) async-start(f32[8,32,256]{2,1,0:T(8,128)} %pack.2), calls=%async_computation.3 | async-start | bytes 524288 | tf_op jit(solution)/shard_map/all_to_all | solution.py:36
  30.4 12.3 %all-to-all-done.3.near_hbm = f32[8,32,256]{2,1,0:T(8,128)} async-done(((f32[8,32,256]{2,1,0:T(8,128)}), f32[8,32,256]{2,1,0:T(8,128)}, u32[]{:S(2)}, u32[]{:S(2)}) %all-to-all-start.3) | async-done | bytes 262176 | tf_op jit(solution)/shard_map/all_to_all | solution.py:36
  42.7 0.6 collective-permute-start.1
  43.3 0.7 while.10
  43.9 0.8 %collective-permute-done.1.far_hbm = f32[8,32,256]{2,1,0:T(8,128)} collective-permute-done((f32[8,32,256]{2,1,0:T(8,128)}, f32[8,32,256]{2,1,0:T(8,128)}, u32[]{:S(2)}, u32[]{:S(2)}) %collective-permute-start.1) | collective-permute-done | bytes 262176 | tf_op jit(solution)/shard_map/ppermute | solution.py:480
  44.8 11.6 %panel.1 = (f32[4096,128]{1,0:T(8,128)}, f32[32,128]{1,0:T(8,128)}, f32[256,128]{1,0:T(8,128)}) custom-call(s32[1]{0:T(128)} %get-tuple-element.156.rounds_ref, f32[8,128]{1,0:T(8,128)} %copy-done.1, f32[128,256]{1,0:T(8,128)} %copy-done, f32[8,32,256]{2,1,0:T(8,128)} %all-to-all-done.3.near_hbm, f32[8,32,256]{2,1,0:T(8,128)} %collective-permute-done.1.far_hbm, ...), custom_call_target="tpu_custom_call" | custom-call | tf_op jit(solution)/shard_map/panel/pallas_call | solution.py:437
  56.4 18.9 %all_to_all.27 = f32[256,1,128]{2,1,0:T(1,128)S(1)} all-to-all(f32[256,1,128]{2,1,0:T(1,128)} %bitcast.49), channel_id=1, replica_groups=mesh['rows'=256] {'rows'}, dimensions={0} | all-to-all | bytes 262144 | tf_op jit(solution)/shard_map/all_to_all | solution.py:36
  75.3 0.9 %slice_reduce_fusion = f32[]{:T(128)} fusion(f32[256,1,128]{2,1,0:T(1,128)S(1)} %all_to_all.27), kind=kLoop, calls=%fused_computation.3 | loop fusion | flops 255 | bytes 1028 | tf_op jit(solution)/shard_map/reduce_sum | solution.py:491
Async XLA Ops:
  3.8 16.3 %all-to-all-start.2 = ((f32[32,8,256]{2,1,0:T(8,128)}), f32[32,8,256]{2,1,0:T(8,128)S(1)}, u32[]{:S(2)}, u32[]{:S(2)}) async-start(f32[32,8,256]{2,1,0:T(8,128)} %bitcast.48), calls=%async_computation.2 | async-start | bytes 524288 | tf_op jit(solution)/shard_map/all_to_all | solution.py:36
  13.6 0.6 copy-start
  14.2 0.6 copy-start.1
  21.1 21.6 %all-to-all-start.3 = ((f32[8,32,256]{2,1,0:T(8,128)}), f32[8,32,256]{2,1,0:T(8,128)}, u32[]{:S(2)}, u32[]{:S(2)}) async-start(f32[8,32,256]{2,1,0:T(8,128)} %pack.2), calls=%async_computation.3 | async-start | bytes 524288 | tf_op jit(solution)/shard_map/all_to_all | solution.py:36
  42.7 2.1 %collective-permute-start.1 = (f32[8,32,256]{2,1,0:T(8,128)}, f32[8,32,256]{2,1,0:T(8,128)}, u32[]{:S(2)}, u32[]{:S(2)}) collective-permute-start(f32[8,32,256]{2,1,0:T(8,128)} %all-to-all-done.3.near_hbm), channel_id=1, source_target_pairs={{0,1},{1,0},{2,3},{3,2},{4,5},{5,4},{6,7},{7,6},{8,9},{9,8},{10,11... | collective-permute-start | bytes 786440 | tf_op jit(solution)/shard_map/ppermute | solution.py:480

commit v4 on v3

--- a/solution.py
+++ b/solution.py
@@ -16,6 +16,7 @@
 HBM = pl.BlockSpec(memory_space=pltpu.HBM)
 NT = (((1,), (1,)), ((), ()))
 SMALL = 16 * 1024 * 1024
+PANEL = 64 * 1024 * 1024 - 840 * 1024
 LAYERS = 8
 RANKS = 8
 SPOTS = 32
@@ -87,20 +88,19 @@
 
     @pl.when(count > 0)
     def _():
-        sub = lax.broadcasted_iota(jnp.int32, (RANKS, 128), 0)
-        lane = lax.broadcasted_iota(jnp.int32, (RANKS, 128), 1)
+        lane = lax.broadcasted_iota(jnp.int32, (feat, 128), 1)
         fac_sub = lax.broadcasted_iota(jnp.int32, prev_part.shape[1:], 0)
-        xs, facs = 0.0, []
+        xs, facs = jnp.zeros((feat, 128), F32), []
         for at in range(RANKS):
             used = at < count
             place = place_of(jnp.where(used, at, 0))
-            only = jnp.where((sub == at) & (lane == lax.rem(place, 128)) & used, 1.0, 0.0)
-            xs = xs + lax.dot_general(only, feat_part[at], NT, precision=HIGH, preferred_element_type=F32)
+            x = jnp.where((lane == lax.rem(place, 128)) & used, feat_part[at], 0.0)
+            xs = jnp.where(lane == at, jnp.sum(x, axis=1, keepdims=True), xs)
             fac = jnp.where((fac_sub == lax.rem(place, 8)) & used, prev_part[at], 0.0)
             facs.append(jnp.sum(fac, axis=0, keepdims=True))
+        xs = jnp.concatenate([xs, jnp.zeros((128 - feat, 128), F32)], axis=0).T[:RANKS]
         facs = jnp.concatenate(facs, axis=0)
-        pad = jnp.zeros((RANKS, 128 - feat), F32)
-        halves = (jnp.concatenate([xs, pad, facs[:, :128]], axis=1), facs[:, 128:])
+        halves = (jnp.concatenate([xs, facs[:, :128]], axis=1), facs[:, 128:])
         for at in range(out_ref.shape[0]):
             for half in range(2):
                 out_ref[at, half] = halves[half]
@@ -203,7 +203,7 @@
 
 
 def pack_kernel(table_ref, rows_ref, out_ref):
-    packed = jnp.dot(table_ref[...], rows_ref[...], precision=HIGH, preferred_element_type=F32)
+    packed = pick_rows(table_ref[...], rows_ref[...])
     for at in range(out_ref.shape[0]):
         out_ref[at] = packed
 
@@ -222,13 +222,13 @@
 def unpack(table, near, far, core):
     first = jnp.where(core == 0, near, far).reshape(LAYERS * SPOTS, 256)
     second = jnp.where(core == 0, far, near).reshape(LAYERS * SPOTS, 256)
-    return jnp.concatenate(
-        [
-            jnp.dot(table, first, precision=HIGH, preferred_element_type=F32),
-            jnp.dot(table, second, precision=HIGH, preferred_element_type=F32),
-        ],
-        axis=1,
-    )
+    return pick_rows(table, jnp.concatenate([first, second], axis=1))
+
+
+def pick_rows(table, rows):
+    table = table.astype(BF16)
+    high, mid, low = [jnp.dot(table, part, preferred_element_type=F32) for part in split3(rows)]
+    return high + mid + low
 
 
 def split2(value):
@@ -250,39 +250,62 @@
     lane = lax.broadcasted_iota(jnp.int32, (8, size), 1)
     sub = lax.broadcasted_iota(jnp.int32, (8, size), 0)
 
-    def spread(value, row):
+    def spread_row(value, row):
         return jnp.broadcast_to(value[row : row + 1], (8, size))
 
+    def spread_columns(value, first):
+        return [jnp.broadcast_to(value[:, first + k : first + k + 1], (8, size)) for k in range(8)]
+
+    diagonal = spread_columns(rows[0], 0)
     for home in range(count):
         first = 8 * home
-        columns = [
-            [jnp.broadcast_to(rows[at][:, first + k : first + k + 1], (8, size)) for at in range(home, count)]
-            for k in range(8)
-        ]
+        more = home + 1 < count
         inside = (lane >= first) & (lane < first + 8)
         top = jnp.where(inside, 0.0, rows[home])
-        factors, pivots, diag = [], [], None
+        pivots, inverses, ahead, pivot_col = [], [], {}, None
+        if more:
+            below = spread_columns(rows[home + 1], first)
+            coming = spread_columns(rows[home + 1], first + 8)
+            below_factors = []
         for step in range(8):
-            pivot = spread(columns[step][0], step)
-            diag = pivot if diag is None else jnp.where(sub == step, pivot, diag)
+            pivot = spread_row(diagonal[step], step)
+            pivot_col = pivot if pivot_col is None else jnp.where(sub == step, pivot, pivot_col)
             inverse = 1.0 / pivot
-            factor = [value * inverse for value in columns[step]]
-            factor[0] = jnp.where(sub > step, factor[0], 0.0)
-            row = jnp.where(lane == first + step, 1.0, spread(top, step))
+            inverses.append(inverse)
+            factor = jnp.where(sub > step, diagonal[step] * inverse, 0.0)
+            for k in range(step + 1, 8):
+                ahead[k, step] = spread_row(diagonal[k], step)
+                diagonal[k] = diagonal[k] - factor * ahead[k, step]
+            if more:
+                part = below[step] * inverse
+                below_factors.append(part)
+                for k in range(step + 1, 8):
+                    below[k] = below[k] - part * ahead[k, step]
+                for k in range(8):
+                    coming[k] = coming[k] - part * spread_row(below[step], k)
+            row = jnp.where(lane == first + step, 1.0, spread_row(top, step))
+            pivots.append(row)
             if step < 7:
-                top = top - factor[0] * row
-                for k in range(step + 1, 8):
-                    ahead = spread(columns[k][0], step)
-                    columns[k] = [value - part * ahead for value, part in zip(columns[k], factor)]
-            factors.append(factor)
-            pivots.append(row)
+                top = top - factor * row
         for at in range(home + 1, count):
+            if at == home + 1:
+                factors = below_factors
+            else:
+                columns = spread_columns(rows[at], first)
+                factors = []
+                for step in range(8):
+                    part = columns[step] * inverses[step]
+                    factors.append(part)
+                    for k in range(step + 1, 8):
+                        columns[k] = columns[k] - part * ahead[k, step]
             value = jnp.where(inside, 0.0, rows[at])
             for step in range(8):
-                value = value - factors[step][at - home] * pivots[step]
+                value = value - factors[step] * pivots[step]
             rows[at] = value
         unit = jnp.where(lane < sub + first, top, 0.0) + jnp.where(lane == sub + first, 1.0, 0.0)
-        result.append(unit * lax.rsqrt(diag))
+        result.append(unit * lax.rsqrt(pivot_col))
+        if more:
+            diagonal = coming
         yield
 
 
@@ -294,22 +317,15 @@
 
 
 def panel_kernel(
-    rounds_ref, aux_hbm, table_hbm, near_hbm, far_hbm, more_hbm, feat_hbm, prev_hbm,
+    rounds_ref, aux_ref, table_ref, near_ref, far_ref, more_hbm, feat_hbm, prev_hbm,
     new_hbm, resid_ref, part_ref,
-    aux_ref, table_ref, near_ref, far_ref, more_ref, feat_ref, prev_ref, cols_ref, squares_ref,
-    first_sems, in_sems, out_sems, *, tile, chunk,
+    more_ref, feat_ref, prev_ref, cols_ref, squares_ref,
+    more_sem, in_sems, out_sems, *, tile, chunk,
 ):
     feat, points = feat_ref.shape
     width = prev_ref.shape[1]
     size = aux_ref.shape[1]
     chunks = points // chunk
-
-    pairs = ((near_hbm, near_ref), (far_hbm, far_ref), (table_hbm, table_ref), (aux_hbm, aux_ref))
-    first_copies = [
-        pltpu.make_async_copy(source, target, first_sems.at[at]) for at, (source, target) in enumerate(pairs)
-    ]
-    for copy in first_copies:
-        copy.start()
 
     def incoming(at):
         here = pl.ds(at * chunk, chunk)
@@ -322,21 +338,19 @@
         here = pl.ds(at * chunk, chunk)
         return pltpu.make_async_copy(cols_ref.at[here, :], new_hbm.at[here, :], out_sems.at[at])
 
+    for at in range(chunks):
+        for copy in incoming(at):
+            copy.start()
+
     @pl.when(rounds_ref[0] > 1)
     def _():
-        copy = pltpu.make_async_copy(more_hbm, more_ref, first_sems.at[len(pairs)])
+        copy = pltpu.make_async_copy(more_hbm, more_ref, more_sem)
         copy.start()
         copy.wait()
 
     @pl.when(rounds_ref[0] <= 1)
     def _():
         more_ref[...] = jnp.zeros_like(more_ref)
-
-    for copy in first_copies:
-        copy.wait()
-    for at in range(chunks):
-        for copy in incoming(at):
-            copy.start()
 
     mine = aux_ref[0:1, :]
     scales_row = aux_ref[1:2, :feat]
@@ -355,20 +369,31 @@
     piv_right = jnp.concatenate([piv_s, pad], axis=1)
     piv_right = jnp.where(lane == feat, -0.5, jnp.where(lane == feat + 1, -0.5 * piv_sq, piv_right))
 
-    row_id = lax.broadcasted_iota(jnp.int32, (size, size), 0)
-    col_id = lax.broadcasted_iota(jnp.int32, (size, size), 1)
-    block = lax.dot_general(piv_left, piv_right, NT, precision=HIGH, preferred_element_type=F32)
-    block = jnp.exp(block) + jnp.where(row_id == col_id, noise, 0.0)
-    block = block - lax.dot_general(piv_f, piv_f, NT, precision=HIGH, preferred_element_type=F32)
-    inverse_rows = []
-    steps = factor_steps(block, inverse_rows)
-
     fac_rhs = stacked(piv_f)
     x_high, x_mid, x_low = split3(piv_right)
     x_rhs = jnp.concatenate(
         [jnp.concatenate([x_high, x_high], axis=1), jnp.concatenate([x_mid, x_mid], axis=1)], axis=0
     )
     x_rest = jnp.concatenate([x_low, x_high], axis=1)
+
+    def kernel_of(left):
+        high, mid, low_part = split3(left)
+        two = lax.dot_general(jnp.concatenate([high, mid], axis=1), x_rhs, NT, preferred_element_type=F32)
+        rest = lax.dot_general(jnp.concatenate([high, low_part], axis=1), x_rest, NT, preferred_element_type=F32)
+        return jnp.exp(two[:, :size] + (two[:, size:] + rest))
+
+    def earlier_of(fac):
+        both = lax.dot_general(
+            jnp.concatenate(split2(fac), axis=1), fac_rhs, NT, preferred_element_type=F32
+        )
+        return both[:, :size] + both[:, size:]
+
+    row_id = lax.broadcasted_iota(jnp.int32, (size, size), 0)
+    col_id = lax.broadcasted_iota(jnp.int32, (size, size), 1)
+    block = kernel_of(piv_left) + jnp.where(row_id == col_id, noise, 0.0) - earlier_of(piv_f)
+    inverse_rows = []
+    steps = factor_steps(block, inverse_rows)
+
     sub = lax.broadcasted_iota(jnp.int32, (8, tile), 0)
     ids = lax.broadcasted_iota(jnp.int32, (tile, size), 0).astype(F32)
 
@@ -378,30 +403,25 @@
         length = jnp.sum(xt * xt * scales_col, axis=0, keepdims=True)
         extra = jnp.where(sub == 0, length, jnp.where(sub == 1, 1.0, 0.0))
         left = jnp.concatenate([xt, extra, jnp.zeros((128 - feat - 8, tile), F32)], axis=0).T
-        high, mid, low_part = split3(left)
-        two = lax.dot_general(jnp.concatenate([high, mid], axis=1), x_rhs, NT, preferred_element_type=F32)
-        rest = lax.dot_general(jnp.concatenate([high, low_part], axis=1), x_rest, NT, preferred_element_type=F32)
-        kern = jnp.exp(two[:, :size] + (two[:, size:] + rest))
-        kern = kern + jnp.where(ids == mine - base, noise, 0.0)
+        kern = kernel_of(left) + jnp.where(ids == mine - base, noise, 0.0)
         fac = prev_ref[here, :]
-        high, low_part = split2(fac)
-        both = lax.dot_general(
-            jnp.concatenate([high, low_part], axis=1), fac_rhs, NT, preferred_element_type=F32
-        )
-        cols_ref[here, :] = kern - (both[:, :size] + both[:, size:])
+        cols_ref[here, :] = kern - earlier_of(fac)
         total = fac[:, :128] * fac[:, :128]
         for start in range(128, width, 128):
             total = total + fac[:, start : start + 128] * fac[:, start : start + 128]
         squares_ref[here, :] = total
 
-    per_chunk = (size // 8) // chunks
-    for at in range(chunks):
-        for copy in incoming(at):
-            copy.wait()
-        for inner in range(chunk // tile):
-            for _ in range(per_chunk * tile // chunk):
-                next(steps)
-            columns(at * chunk + inner * tile)
+    for _ in range(3):
+        next(steps, None)
+    done = 0
+    for at in range(points // tile):
+        if at in (0, 6):
+            for part in range({0: 3, 6: 5}[at]):
+                for copy in incoming(done):
+                    copy.wait()
+                done += 1
+        columns(at * tile)
+        next(steps, None)
     for _ in steps:
         pass
 
@@ -441,23 +461,19 @@
             jax.ShapeDtypeStruct((points // 128, 128), F32),
             jax.ShapeDtypeStruct((devices, 128), F32),
         ),
-        in_specs=[SMEM] + [ANY] * 7,
+        in_specs=[SMEM] + [VMEM] * 4 + [ANY] * 3,
         out_specs=(ANY, VMEM, VMEM),
         scratch_shapes=[
-            pltpu.VMEM(aux.shape, F32),
-            pltpu.VMEM(table.shape, F32),
-            pltpu.VMEM(near.shape, F32),
-            pltpu.VMEM(far.shape, F32),
             pltpu.VMEM(more.shape, F32),
             pltpu.VMEM((feat, points), F32),
             pltpu.VMEM((points, width), F32),
             pltpu.VMEM((points, size), F32),
             pltpu.VMEM((points, 128), F32),
-            pltpu.SemaphoreType.DMA((5,)),
+            pltpu.SemaphoreType.DMA,
             pltpu.SemaphoreType.DMA((2, points // chunk)),
             pltpu.SemaphoreType.DMA((points // chunk,)),
         ],
-        compiler_params=pltpu.CompilerParams(vmem_limit_bytes=64 * 1024 * 1024),
+        compiler_params=pltpu.CompilerParams(vmem_limit_bytes=PANEL),
         name="panel",
     )(rounds, aux, table, near, far, more, feat_t, prev)
 

time: 76.2 us -> 75.1 us (0.986)
  Pallas kernels: 17.6 us -> 16.2 us
    pallas_call x1, Pallas kernels: 11.6 us -> 10.6 us  [run_panel(): pl.pallas_call(functools.partial(panel_kernel, tile=256, chunk=chunk), ou...]
where the time goes in v4:
time: 75.1 us; the launch traced here: 75 us
  blocking collectives  18.9 us (25%)
  waiting for transfers between devices  18.5 us (25%)
  starting transfers between devices  17.4 us (23%)
  Pallas kernels  16.2 us (22%)
  between operations  1.33 us (2%)
  local copies, waits for them, and re-layouts  1.23 us (2%)
  other arithmetic  0.87 us (1%)
    all_to_all x1, blocking collectives, exchange(): lax.all_to_all(blocks, 'rows', 0, 0, axis_index_groups=groups, tiled=True)  18.9 us
    all_to_all x2, waiting for transfers between devices, exchange(): lax.all_to_all(blocks, 'rows', 0, 0, axis_index_groups=groups, tiled=True)  17.6 us
    all_to_all x2, starting transfers between devices, exchange(): lax.all_to_all(blocks, 'rows', 0, 0, axis_index_groups=groups, tiled=True)  16.8 us
    pallas_call x1, Pallas kernels, run_panel(): pl.pallas_call(functools.partial(panel_kernel, tile=256, chunk=chunk), ou...  10.6 us
    pallas_call x1, Pallas kernels, run_pick(): pl.pallas_call(pick_kernel, out_shape=jax.ShapeDtypeStruct((16, 2, RANKS,...  2.88 us
    pallas_call x1, Pallas kernels, run_table(): pl.pallas_call(table_kernel, out_shape=(jax.ShapeDtypeStruct((SPOTS, 32 *...  1.81 us
  transfers between devices with their start and end apart: 3, of which 3 were waited for; matrix products, arithmetic and copies ran while one was open for 0% of the time, Pallas kernels for 2%

profile of v4, /device:TPU:1, one launch (start us, length us, event | category | flops | bytes accessed | tf_op | source)
XLA Modules:
  0.0 75.0 jit_solution(6355827121240189589)
XLA Ops:
  0.6 2.9 %pick.2 = f32[16,2,8,256]{3,2,1,0:T(8,128)} custom-call(s32[1]{0:T(128)} %constant.3.clone.1.round_ref, s32[2,64]{1,0:T(2,128)} %owner_hbm.1, s32[2,64]{1,0:T(2,128)} %place_hbm.1, f32[64,4096]{1,0:T(8,128)} %bitcast.37, f32[4096,384]{1,0:T(8,128)} %prev_hbm.3), custom_call_target="tpu_custom_call" | custom-call | tf_op jit(solution)/shard_map/pick/pallas_call | solution.py:114
  3.5 7.6 %all-to-all-start.2 = ((f32[32,8,256]{2,1,0:T(8,128)}), f32[32,8,256]{2,1,0:T(8,128)S(1)}, u32[]{:S(2)}, u32[]{:S(2)}) async-start(f32[32,8,256]{2,1,0:T(8,128)} %bitcast.40), calls=%async_computation.2 | async-start | bytes 524288 | tf_op jit(solution)/shard_map/all_to_all | solution.py:37
  11.8 1.8 %table.2 = (f32[32,256]{1,0:T(8,128)S(1)}, f32[128,256]{1,0:T(8,128)S(1)}, f32[8,128]{1,0:T(8,128)S(1)}, f32[128,512]{1,0:T(8,128)}, s32[1]{0:T(128)}) custom-call(s32[1]{0:T(128)} %constant.3.clone.1.round_ref, f32[1]{0:T(128)S(6)} %copy.16.noise_ref, s32[2,64]{1,0:T(2,128)} %owner_hbm.1, s32[2,64]{1,0:T(2,128)} %place_hbm.1, f32[1,64]{1,0:T(1,128)} %bitcast.42), custom_call_target="tpu_custom_call" | custom-call | tf_op jit(solution)/shard_map/table/pallas_call | solution.py:189
  13.6 0.0 copy-start
  13.6 0.6 copy-done
  14.2 0.0 copy-start.1
  14.2 0.6 copy-done.1
  14.8 5.3 %all-to-all-done.2 = f32[32,8,256]{2,1,0:T(8,128)S(1)} async-done(((f32[32,8,256]{2,1,0:T(8,128)}), f32[32,8,256]{2,1,0:T(8,128)S(1)}, u32[]{:S(2)}, u32[]{:S(2)}) %all-to-all-start.2) | async-done | bytes 262176 | tf_op jit(solution)/shard_map/all_to_all | solution.py:37
  20.1 0.9 %pack.2 = f32[8,32,256]{2,1,0:T(8,128)} custom-call(f32[32,256]{1,0:T(8,128)S(1)} %get-tuple-element.64.table_ref, f32[256,256]{1,0:T(8,128)S(1)} %bitcast.30), custom_call_target="tpu_custom_call" | custom-call | tf_op jit(solution)/shard_map/pack/pallas_call | solution.py:212
  21.0 9.2 %all-to-all-start.3 = ((f32[8,32,256]{2,1,0:T(8,128)}), f32[8,32,256]{2,1,0:T(8,128)}, u32[]{:S(2)}, u32[]{:S(2)}) async-start(f32[8,32,256]{2,1,0:T(8,128)} %pack.2), calls=%async_computation.3 | async-start | bytes 524288 | tf_op jit(solution)/shard_map/all_to_all | solution.py:37
  30.2 12.3 %all-to-all-done.3.near_ref = f32[8,32,256]{2,1,0:T(8,128)} async-done(((f32[8,32,256]{2,1,0:T(8,128)}), f32[8,32,256]{2,1,0:T(8,128)}, u32[]{:S(2)}, u32[]{:S(2)}) %all-to-all-start.3) | async-done | bytes 262176 | tf_op jit(solution)/shard_map/all_to_all | solution.py:37
  42.6 0.6 collective-permute-start.1
  43.2 0.7 while.10
  43.8 0.8 %collective-permute-done.1.far_ref = f32[8,32,256]{2,1,0:T(8,128)} collective-permute-done((f32[8,32,256]{2,1,0:T(8,128)}, f32[8,32,256]{2,1,0:T(8,128)}, u32[]{:S(2)}, u32[]{:S(2)}) %collective-permute-start.1) | collective-permute-done | bytes 262176 | tf_op jit(solution)/shard_map/ppermute | solution.py:496
  44.7 10.6 %panel.1 = (f32[4096,128]{1,0:T(8,128)}, f32[32,128]{1,0:T(8,128)}, f32[256,128]{1,0:T(8,128)}) custom-call(s32[1]{0:T(128)} %get-tuple-element.156.rounds_ref, f32[8,128]{1,0:T(8,128)} %copy-done.1, f32[128,256]{1,0:T(8,128)} %copy-done, f32[8,32,256]{2,1,0:T(8,128)} %all-to-all-done.3.near_ref, f32[8,32,256]{2,1,0:T(8,128)} %collective-permute-done.1.far_ref, ...), custom_call_target="tpu_custom_call" | custom-call | tf_op jit(solution)/shard_map/panel/pallas_call | solution.py:457
  55.2 18.9 %all_to_all.27 = f32[256,1,128]{2,1,0:T(1,128)S(1)} all-to-all(f32[256,1,128]{2,1,0:T(1,128)} %bitcast.41), channel_id=1, replica_groups=mesh['rows'=256] {'rows'}, dimensions={0} | all-to-all | bytes 262144 | tf_op jit(solution)/shard_map/all_to_all | solution.py:37
  74.2 0.9 %slice_reduce_fusion = f32[]{:T(128)} fusion(f32[256,1,128]{2,1,0:T(1,128)S(1)} %all_to_all.27), kind=kLoop, calls=%fused_computation.17 | loop fusion | flops 255 | bytes 1028 | tf_op jit(solution)/shard_map/reduce_sum | solution.py:507
Async XLA Ops:
  3.5 16.6 %all-to-all-start.2 = ((f32[32,8,256]{2,1,0:T(8,128)}), f32[32,8,256]{2,1,0:T(8,128)S(1)}, u32[]{:S(2)}, u32[]{:S(2)}) async-start(f32[32,8,256]{2,1,0:T(8,128)} %bitcast.40), calls=%async_computation.2 | async-start | bytes 524288 | tf_op jit(solution)/shard_map/all_to_all | solution.py:37
  13.6 0.6 copy-start
  14.2 0.6 copy-start.1
  21.0 21.5 %all-to-all-start.3 = ((f32[8,32,256]{2,1,0:T(8,128)}), f32[8,32,256]{2,1,0:T(8,128)}, u32[]{:S(2)}, u32[]{:S(2)}) async-start(f32[8,32,256]{2,1,0:T(8,128)} %pack.2), calls=%async_computation.3 | async-start | bytes 524288 | tf_op jit(solution)/shard_map/all_to_all | solution.py:37
  42.6 2.1 %collective-permute-start.1 = (f32[8,32,256]{2,1,0:T(8,128)}, f32[8,32,256]{2,1,0:T(8,128)}, u32[]{:S(2)}, u32[]{:S(2)}) collective-permute-start(f32[8,32,256]{2,1,0:T(8,128)} %all-to-all-done.3.near_ref), channel_id=1, source_target_pairs={{0,1},{1,0},{2,3},{3,2},{4,5},{5,4},{6,7},{7,6},{8,9},{9,8},{10,11... | collective-permute-start | bytes 786440 | tf_op jit(solution)/shard_map/ppermute | solution.py:496

commit v5 on v4

--- a/solution.py
+++ b/solution.py
@@ -16,7 +16,7 @@
 HBM = pl.BlockSpec(memory_space=pltpu.HBM)
 NT = (((1,), (1,)), ((), ()))
 SMALL = 16 * 1024 * 1024
-PANEL = 64 * 1024 * 1024 - 840 * 1024
+PANEL = 60000000
 LAYERS = 8
 RANKS = 8
 SPOTS = 32
@@ -309,6 +309,21 @@
         yield
 
 
+def halved_steps(block, result):
+    half = block.shape[0] // 2
+    upper, lower = [], []
+    yield from factor_steps(block[:half, :half], upper)
+    upper = jnp.concatenate(upper, axis=0)
+    joint = lax.dot_general(block[half:, :half], upper, NT, precision=HIGH, preferred_element_type=F32)
+    rest = lax.dot_general(joint, joint, NT, precision=HIGH, preferred_element_type=F32)
+    joint = jnp.dot(joint, upper, precision=HIGH, preferred_element_type=F32)
+    yield from factor_steps(block[half:, half:] - rest, lower)
+    lower = jnp.concatenate(lower, axis=0)
+    joint = jnp.dot(lower, joint, precision=HIGH, preferred_element_type=F32)
+    result.append(jnp.concatenate([upper, jnp.zeros_like(upper)], axis=1))
+    result.append(jnp.concatenate([-joint, lower], axis=1))
+
+
 def stacked(value):
     high, low = split2(value)
     return jnp.concatenate(
@@ -392,7 +407,7 @@
     col_id = lax.broadcasted_iota(jnp.int32, (size, size), 1)
     block = kernel_of(piv_left) + jnp.where(row_id == col_id, noise, 0.0) - earlier_of(piv_f)
     inverse_rows = []
-    steps = factor_steps(block, inverse_rows)
+    steps = halved_steps(block, inverse_rows)
 
     sub = lax.broadcasted_iota(jnp.int32, (8, tile), 0)
     ids = lax.broadcasted_iota(jnp.int32, (tile, size), 0).astype(F32)
@@ -411,7 +426,7 @@
             total = total + fac[:, start : start + 128] * fac[:, start : start + 128]
         squares_ref[here, :] = total
 
-    for _ in range(3):
+    for _ in range(5):
         next(steps, None)
     done = 0
     for at in range(points // tile):

time: 75.1 us -> 74.8 us (level); the launches traced: 75 us -> 73.8 us
  starting transfers between devices: 17.4 us -> 16.2 us
    all_to_all x2, starting transfers between devices: 16.8 us -> 15.6 us  [exchange(): lax.all_to_all(blocks, 'rows', 0, 0, axis_index_groups=groups, tiled=True)]
where the time goes in v5:
time: 74.8 us; the launch traced here: 73.8 us
  blocking collectives  18.9 us (25%)
  waiting for transfers between devices  18.5 us (25%)
  starting transfers between devices  16.2 us (22%)
  Pallas kernels  16.1 us (22%)
  between operations  1.33 us (2%)
  local copies, waits for them, and re-layouts  1.23 us (2%)
  other arithmetic  0.87 us (1%)
    all_to_all x1, blocking collectives, exchange(): lax.all_to_all(blocks, 'rows', 0, 0, axis_index_groups=groups, tiled=True)  18.9 us
    all_to_all x2, waiting for transfers between devices, exchange(): lax.all_to_all(blocks, 'rows', 0, 0, axis_index_groups=groups, tiled=True)  17.6 us
    all_to_all x2, starting transfers between devices, exchange(): lax.all_to_all(blocks, 'rows', 0, 0, axis_index_groups=groups, tiled=True)  15.6 us
    pallas_call x1, Pallas kernels, run_panel(): pl.pallas_call(functools.partial(panel_kernel, tile=256, chunk=chunk), ou...  10.3 us
    pallas_call x1, Pallas kernels, run_pick(): pl.pallas_call(pick_kernel, out_shape=jax.ShapeDtypeStruct((16, 2, RANKS,...  3.02 us
    pallas_call x1, Pallas kernels, run_table(): pl.pallas_call(table_kernel, out_shape=(jax.ShapeDtypeStruct((SPOTS, 32 *...  1.81 us
  transfers between devices with their start and end apart: 3, of which 3 were waited for; matrix products, arithmetic and copies ran while one was open for 0% of the time, Pallas kernels for 2%

profile of v5, /device:TPU:1, one launch (start us, length us, event | category | flops | bytes accessed | tf_op | source)
XLA Modules:
  0.0 73.8 jit_solution(2807486131372885050)
XLA Ops:
  0.6 3.0 %pick.2 = f32[16,2,8,256]{3,2,1,0:T(8,128)} custom-call(s32[1]{0:T(128)} %constant.3.clone.1.round_ref, s32[2,64]{1,0:T(2,128)} %owner_hbm.1, s32[2,64]{1,0:T(2,128)} %place_hbm.1, f32[64,4096]{1,0:T(8,128)} %bitcast.37, f32[4096,384]{1,0:T(8,128)} %prev_hbm.3), custom_call_target="tpu_custom_call" | custom-call | tf_op jit(solution)/shard_map/pick/pallas_call | solution.py:114
  3.7 7.8 %all-to-all-start.2 = ((f32[32,8,256]{2,1,0:T(8,128)}), f32[32,8,256]{2,1,0:T(8,128)S(1)}, u32[]{:S(2)}, u32[]{:S(2)}) async-start(f32[32,8,256]{2,1,0:T(8,128)} %bitcast.40), calls=%async_computation.2 | async-start | bytes 524288 | tf_op jit(solution)/shard_map/all_to_all | solution.py:37
  12.1 1.8 %table.2 = (f32[32,256]{1,0:T(8,128)S(1)}, f32[128,256]{1,0:T(8,128)S(1)}, f32[8,128]{1,0:T(8,128)S(1)}, f32[128,512]{1,0:T(8,128)}, s32[1]{0:T(128)}) custom-call(s32[1]{0:T(128)} %constant.3.clone.1.round_ref, f32[1]{0:T(128)S(6)} %copy.16.noise_ref, s32[2,64]{1,0:T(2,128)} %owner_hbm.1, s32[2,64]{1,0:T(2,128)} %place_hbm.1, f32[1,64]{1,0:T(1,128)} %bitcast.42), custom_call_target="tpu_custom_call" | custom-call | tf_op jit(solution)/shard_map/table/pallas_call | solution.py:189
  13.9 0.0 copy-start
  13.9 0.6 copy-done
  14.5 0.0 copy-start.1
  14.5 0.6 copy-done.1
  15.1 5.3 %all-to-all-done.2 = f32[32,8,256]{2,1,0:T(8,128)S(1)} async-done(((f32[32,8,256]{2,1,0:T(8,128)}), f32[32,8,256]{2,1,0:T(8,128)S(1)}, u32[]{:S(2)}, u32[]{:S(2)}) %all-to-all-start.2) | async-done | bytes 262176 | tf_op jit(solution)/shard_map/all_to_all | solution.py:37
  20.4 0.9 %pack.2 = f32[8,32,256]{2,1,0:T(8,128)} custom-call(f32[32,256]{1,0:T(8,128)S(1)} %get-tuple-element.64.table_ref, f32[256,256]{1,0:T(8,128)S(1)} %bitcast.30), custom_call_target="tpu_custom_call" | custom-call | tf_op jit(solution)/shard_map/pack/pallas_call | solution.py:212
  21.3 7.9 %all-to-all-start.3 = ((f32[8,32,256]{2,1,0:T(8,128)}), f32[8,32,256]{2,1,0:T(8,128)}, u32[]{:S(2)}, u32[]{:S(2)}) async-start(f32[8,32,256]{2,1,0:T(8,128)} %pack.2), calls=%async_computation.3 | async-start | bytes 524288 | tf_op jit(solution)/shard_map/all_to_all | solution.py:37
  29.2 12.3 %all-to-all-done.3.near_ref = f32[8,32,256]{2,1,0:T(8,128)} async-done(((f32[8,32,256]{2,1,0:T(8,128)}), f32[8,32,256]{2,1,0:T(8,128)}, u32[]{:S(2)}, u32[]{:S(2)}) %all-to-all-start.3) | async-done | bytes 262176 | tf_op jit(solution)/shard_map/all_to_all | solution.py:37
  41.6 0.6 collective-permute-start.1
  42.2 0.7 while.10
  42.8 0.8 %collective-permute-done.1.far_ref = f32[8,32,256]{2,1,0:T(8,128)} collective-permute-done((f32[8,32,256]{2,1,0:T(8,128)}, f32[8,32,256]{2,1,0:T(8,128)}, u32[]{:S(2)}, u32[]{:S(2)}) %collective-permute-start.1) | collective-permute-done | bytes 262176 | tf_op jit(solution)/shard_map/ppermute | solution.py:511
  43.7 10.3 %panel.1 = (f32[4096,128]{1,0:T(8,128)}, f32[32,128]{1,0:T(8,128)}, f32[256,128]{1,0:T(8,128)}) custom-call(s32[1]{0:T(128)} %get-tuple-element.156.rounds_ref, f32[8,128]{1,0:T(8,128)} %copy-done.1, f32[128,256]{1,0:T(8,128)} %copy-done, f32[8,32,256]{2,1,0:T(8,128)} %all-to-all-done.3.near_ref, f32[8,32,256]{2,1,0:T(8,128)} %collective-permute-done.1.far_ref, ...), custom_call_target="tpu_custom_call" | custom-call | tf_op jit(solution)/shard_map/panel/pallas_call | solution.py:472
  54.0 18.9 %all_to_all.27 = f32[256,1,128]{2,1,0:T(1,128)S(1)} all-to-all(f32[256,1,128]{2,1,0:T(1,128)} %bitcast.41), channel_id=1, replica_groups=mesh['rows'=256] {'rows'}, dimensions={0} | all-to-all | bytes 262144 | tf_op jit(solution)/shard_map/all_to_all | solution.py:37
  72.9 0.9 %slice_reduce_fusion = f32[]{:T(128)} fusion(f32[256,1,128]{2,1,0:T(1,128)S(1)} %all_to_all.27), kind=kLoop, calls=%fused_computation.17 | loop fusion | flops 255 | bytes 1028 | tf_op jit(solution)/shard_map/reduce_sum | solution.py:522
Async XLA Ops:
  3.7 16.7 %all-to-all-start.2 = ((f32[32,8,256]{2,1,0:T(8,128)}), f32[32,8,256]{2,1,0:T(8,128)S(1)}, u32[]{:S(2)}, u32[]{:S(2)}) async-start(f32[32,8,256]{2,1,0:T(8,128)} %bitcast.40), calls=%async_computation.2 | async-start | bytes 524288 | tf_op jit(solution)/shard_map/all_to_all | solution.py:37
  13.9 0.6 copy-start
  14.5 0.6 copy-start.1
  21.3 20.2 %all-to-all-start.3 = ((f32[8,32,256]{2,1,0:T(8,128)}), f32[8,32,256]{2,1,0:T(8,128)}, u32[]{:S(2)}, u32[]{:S(2)}) async-start(f32[8,32,256]{2,1,0:T(8,128)} %pack.2), calls=%async_computation.3 | async-start | bytes 524288 | tf_op jit(solution)/shard_map/all_to_all | solution.py:37
  41.6 2.1 %collective-permute-start.1 = (f32[8,32,256]{2,1,0:T(8,128)}, f32[8,32,256]{2,1,0:T(8,128)}, u32[]{:S(2)}, u32[]{:S(2)}) collective-permute-start(f32[8,32,256]{2,1,0:T(8,128)} %all-to-all-done.3.near_ref), channel_id=1, source_target_pairs={{0,1},{1,0},{2,3},{3,2},{4,5},{5,4},{6,7},{7,6},{8,9},{9,8},{10,11... | collective-permute-start | bytes 786440 | tf_op jit(solution)/shard_map/ppermute | solution.py:511

commit v6 on v5

--- a/solution.py
+++ b/solution.py
@@ -17,6 +17,7 @@
 NT = (((1,), (1,)), ((), ()))
 SMALL = 16 * 1024 * 1024
 PANEL = 60000000
+ROUNDS = 64
 LAYERS = 8
 RANKS = 8
 SPOTS = 32
@@ -170,7 +171,9 @@
     split = whole(spot, SPOTS)
     spot = rest(spot, SPOTS)
     active = (window == window_now) & (split == split_now)
-    rounds_ref[0] = jnp.max(window * SPLITS + split).astype(jnp.int32) + 1
+    number = window * SPLITS + split
+    later = number > at_round.astype(F32)
+    rounds_ref[0] = jnp.min(jnp.where(later, number, float(ROUNDS))).astype(jnp.int32)
 
     wide = lax.broadcasted_iota(jnp.int32, (size, LAYERS * SPOTS), 1).astype(F32)
     both = lambda value: jnp.concatenate([value, value], axis=1)
@@ -357,13 +360,13 @@
         for copy in incoming(at):
             copy.start()
 
-    @pl.when(rounds_ref[0] > 1)
+    @pl.when(rounds_ref[0] < ROUNDS)
     def _():
         copy = pltpu.make_async_copy(more_hbm, more_ref, more_sem)
         copy.start()
         copy.wait()
 
-    @pl.when(rounds_ref[0] <= 1)
+    @pl.when(rounds_ref[0] >= ROUNDS)
     def _():
         more_ref[...] = jnp.zeros_like(more_ref)
 
@@ -512,11 +515,11 @@
 
     def again(carry):
         at_round, more = carry
-        table, near, far, *_ = fetch(at_round.reshape(1))
-        return at_round + 1, more + unpack(table, near, far, lax.rem(lax.axis_index("rows"), 2))
+        table, near, far, _, _, coming = fetch(at_round)
+        return coming, more + unpack(table, near, far, lax.rem(lax.axis_index("rows"), 2))
 
     table, near, far, aux, more, rounds = fetch(jnp.zeros((1,), jnp.int32))
-    _, more = lax.while_loop(lambda carry: carry[0] < rounds[0], again, (jnp.int32(1), more))
+    _, more = lax.while_loop(lambda carry: carry[0][0] < ROUNDS, again, (rounds, more))
     new_factors, resid, part = run_panel(devices, rounds, aux, table, near, far, more, feat_t, prev_factors)
     sums = exchange(part.reshape(devices, 1, 128), None)
     trace = jnp.sum(sums[:, 0, 0]).reshape(1)

time: 74.8 us -> 74.9 us (level)
  no operation moved by 1% of the time
where the time goes in v6:
time: 74.9 us; the launch traced here: 74.3 us
  blocking collectives  18.9 us (25%)
  waiting for transfers between devices  18.5 us (25%)
  starting transfers between devices  16.8 us (22%)
  Pallas kernels  16 us (21%)
  between operations  1.97 us (3%)
  local copies, waits for them, and re-layouts  1.23 us (2%)
  other arithmetic  0.87 us (1%)
    all_to_all x1, blocking collectives, exchange(): lax.all_to_all(blocks, 'rows', 0, 0, axis_index_groups=groups, tiled=True)  18.9 us
    all_to_all x2, waiting for transfers between devices, exchange(): lax.all_to_all(blocks, 'rows', 0, 0, axis_index_groups=groups, tiled=True)  17 us
    all_to_all x2, starting transfers between devices, exchange(): lax.all_to_all(blocks, 'rows', 0, 0, axis_index_groups=groups, tiled=True)  16.2 us
    pallas_call x1, Pallas kernels, run_panel(): pl.pallas_call(functools.partial(panel_kernel, tile=256, chunk=chunk), ou...  10.3 us
    pallas_call x1, Pallas kernels, run_pick(): pl.pallas_call(pick_kernel, out_shape=jax.ShapeDtypeStruct((16, 2, RANKS,...  2.92 us
    pallas_call x1, Pallas kernels, run_table(): pl.pallas_call(table_kernel, out_shape=(jax.ShapeDtypeStruct((SPOTS, 32 *...  1.81 us
    ppermute x1, waiting for transfers between devices, fetch(): return (table, near, lax.ppermute(near, 'rows', cores), aux, more, rounds)  1.5 us
  transfers between devices with their start and end apart: 3, of which 3 were waited for; matrix products, arithmetic and copies ran while one was open for 0% of the time, Pallas kernels for 2%

profile of v6, /device:TPU:1, one launch (start us, length us, event | category | flops | bytes accessed | tf_op | source)
XLA Modules:
  0.0 74.3 jit_solution(8866905962618254846)
XLA Ops:
  0.6 2.9 %pick.2 = f32[16,2,8,256]{3,2,1,0:T(8,128)} custom-call(s32[1]{0:T(128)} %constant.15.clone.1.round_ref, s32[2,64]{1,0:T(2,128)} %owner_hbm.1, s32[2,64]{1,0:T(2,128)} %place_hbm.1, f32[64,4096]{1,0:T(8,128)} %bitcast.34, f32[4096,384]{1,0:T(8,128)} %prev_hbm.3), custom_call_target="tpu_custom_call" | custom-call | tf_op jit(solution)/shard_map/pick/pallas_call | solution.py:115
  3.6 8.0 %all-to-all-start.2 = ((f32[32,8,256]{2,1,0:T(8,128)}), f32[32,8,256]{2,1,0:T(8,128)S(1)}, u32[]{:S(2)}, u32[]{:S(2)}) async-start(f32[32,8,256]{2,1,0:T(8,128)} %bitcast.37), calls=%async_computation.2 | async-start | bytes 524288 | tf_op jit(solution)/shard_map/all_to_all | solution.py:38
  12.2 1.8 %table.2 = (f32[32,256]{1,0:T(8,128)S(1)}, f32[128,256]{1,0:T(8,128)S(1)}, f32[8,128]{1,0:T(8,128)S(1)}, f32[128,512]{1,0:T(8,128)}, s32[1]{0:T(128)}) custom-call(s32[1]{0:T(128)} %constant.15.clone.1.round_ref, f32[1]{0:T(128)S(6)} %copy.16.noise_ref, s32[2,64]{1,0:T(2,128)} %owner_hbm.1, s32[2,64]{1,0:T(2,128)} %place_hbm.1, f32[1,64]{1,0:T(1,128)} %bitcast.39), custom_call_target="tpu_custom_call" | custom-call | tf_op jit(solution)/shard_map/table/pallas_call | solution.py:192
  14.0 0.0 copy-start
  14.0 0.6 copy-done
  14.7 0.0 copy-start.1
  14.7 0.6 copy-done.1
  15.3 5.3 %all-to-all-done.2 = f32[32,8,256]{2,1,0:T(8,128)S(1)} async-done(((f32[32,8,256]{2,1,0:T(8,128)}), f32[32,8,256]{2,1,0:T(8,128)S(1)}, u32[]{:S(2)}, u32[]{:S(2)}) %all-to-all-start.2) | async-done | bytes 262176 | tf_op jit(solution)/shard_map/all_to_all | solution.py:38
  20.6 0.9 %pack.2 = f32[8,32,256]{2,1,0:T(8,128)} custom-call(f32[32,256]{1,0:T(8,128)S(1)} %get-tuple-element.59.table_ref, f32[256,256]{1,0:T(8,128)S(1)} %bitcast.27), custom_call_target="tpu_custom_call" | custom-call | tf_op jit(solution)/shard_map/pack/pallas_call | solution.py:215
  21.5 8.2 %all-to-all-start.3 = ((f32[8,32,256]{2,1,0:T(8,128)}), f32[8,32,256]{2,1,0:T(8,128)}, u32[]{:S(2)}, u32[]{:S(2)}) async-start(f32[8,32,256]{2,1,0:T(8,128)} %pack.2), calls=%async_computation.3 | async-start | bytes 524288 | tf_op jit(solution)/shard_map/all_to_all | solution.py:38
  30.3 11.7 %all-to-all-done.3.near_ref = f32[8,32,256]{2,1,0:T(8,128)} async-done(((f32[8,32,256]{2,1,0:T(8,128)}), f32[8,32,256]{2,1,0:T(8,128)}, u32[]{:S(2)}, u32[]{:S(2)}) %all-to-all-start.3) | async-done | bytes 262176 | tf_op jit(solution)/shard_map/all_to_all | solution.py:38
  42.0 0.6 collective-permute-start.1
  42.6 1.5 %collective-permute-done.1.far_ref = f32[8,32,256]{2,1,0:T(8,128)} collective-permute-done((f32[8,32,256]{2,1,0:T(8,128)}, f32[8,32,256]{2,1,0:T(8,128)}, u32[]{:S(2)}, u32[]{:S(2)}) %collective-permute-start.1) | collective-permute-done | bytes 262176 | tf_op jit(solution)/shard_map/ppermute | solution.py:514
  44.1 10.3 %panel.1 = (f32[4096,128]{1,0:T(8,128)}, f32[32,128]{1,0:T(8,128)}, f32[256,128]{1,0:T(8,128)}) custom-call(s32[1]{0:T(128)} %get-tuple-element.142.rounds_ref, f32[8,128]{1,0:T(8,128)} %copy-done.1, f32[128,256]{1,0:T(8,128)} %copy-done, f32[8,32,256]{2,1,0:T(8,128)} %all-to-all-done.3.near_ref, f32[8,32,256]{2,1,0:T(8,128)} %collective-permute-done.1.far_ref, ...), custom_call_target="tpu_custom_call" | custom-call | tf_op jit(solution)/shard_map/panel/pallas_call | solution.py:475
  54.5 18.9 %all_to_all.27 = f32[256,1,128]{2,1,0:T(1,128)S(1)} all-to-all(f32[256,1,128]{2,1,0:T(1,128)} %bitcast.38), channel_id=1, replica_groups=mesh['rows'=256] {'rows'}, dimensions={0} | all-to-all | bytes 262144 | tf_op jit(solution)/shard_map/all_to_all | solution.py:38
  73.4 0.9 %slice_reduce_fusion = f32[]{:T(128)} fusion(f32[256,1,128]{2,1,0:T(1,128)S(1)} %all_to_all.27), kind=kLoop, calls=%fused_computation.17 | loop fusion | flops 255 | bytes 1028 | tf_op jit(solution)/shard_map/reduce_sum | solution.py:525
  (1 shorter events, 0.0 us)
Async XLA Ops:
  3.6 17.0 %all-to-all-start.2 = ((f32[32,8,256]{2,1,0:T(8,128)}), f32[32,8,256]{2,1,0:T(8,128)S(1)}, u32[]{:S(2)}, u32[]{:S(2)}) async-start(f32[32,8,256]{2,1,0:T(8,128)} %bitcast.37), calls=%async_computation.2 | async-start | bytes 524288 | tf_op jit(solution)/shard_map/all_to_all | solution.py:38
  14.0 0.6 copy-start
  14.7 0.6 copy-start.1
  21.5 20.5 %all-to-all-start.3 = ((f32[8,32,256]{2,1,0:T(8,128)}), f32[8,32,256]{2,1,0:T(8,128)}, u32[]{:S(2)}, u32[]{:S(2)}) async-start(f32[8,32,256]{2,1,0:T(8,128)} %pack.2), calls=%async_computation.3 | async-start | bytes 524288 | tf_op jit(solution)/shard_map/all_to_all | solution.py:38
  42.0 2.1 %collective-permute-start.1 = (f32[8,32,256]{2,1,0:T(8,128)}, f32[8,32,256]{2,1,0:T(8,128)}, u32[]{:S(2)}, u32[]{:S(2)}) collective-permute-start(f32[8,32,256]{2,1,0:T(8,128)} %all-to-all-done.3.near_ref), channel_id=1, source_target_pairs={{0,1},{1,0},{2,3},{3,2},{4,5},{5,4},{6,7},{7,6},{8,9},{9,8},{10,11... | collective-permute-start | bytes 786440 | tf_op jit(solution)/shard_map/ppermute | solution.py:514
